TPU v7x, 256 devices: a whole 4x4x8 slice. The times are simulated.
256 devices in a mesh: grid: 32 (over x, y, z_lo), orb: 8 (over z_hi, core).
Axes of the slice: x: 4, y: 4, z: 8 (z_hi: 4, z_lo: 2; z = z_hi * 2 + z_lo), core: 2. Of those that a mesh axis runs over, the one named last changes fastest.
Arguments:
- orbitals: float32 [512, 128, 8, 128], P('orb', 'grid'), may hold values from -13 to 13, as said below
- potential: float32 [128, 8, 128], P('grid'), may hold values from -1 to 1
Outputs:
- orthonormal: float32 [512, 128, 8, 128], P('orb', 'grid')
Inputs may be any that keep to these rules, and one draw needn't show every extreme that they name: Trial orbitals, real-valued.
All inputs are finite; a program needn't handle non-finite values.
Results may differ from a plain program's by a relative error of at most 0.0003.
Values sent between devices are 32-bit elements; how exact they have to be, the bound alone decides.
A program may use at most 64 MiB of HBM per device.

v0:
```python
import jax
import jax.numpy as jnp
from jax import lax
from jax.sharding import PartitionSpec as P

lap_weights = (-205.0 / 72.0, 8.0 / 5.0, -1.0 / 5.0, 8.0 / 315.0, -1.0 / 560.0)
lower_edge = 3.0
upper_edge = 11.0


def padded_2(cells, sides, width):
    for axis, dim in sides:
        count = lax.axis_size(axis)
        head = lax.slice_in_dim(cells, 0, width, axis=dim)
        tail = lax.slice_in_dim(cells, cells.shape[dim] - width, cells.shape[dim], axis=dim)
        cells = jnp.concatenate(
            [
                lax.ppermute(tail, axis, [(i, (i + 1) % count) for i in range(count)]),
                cells,
                lax.ppermute(head, axis, [((i + 1) % count, i) for i in range(count)]),
            ],
            axis=dim,
        )
    return cells


def wrap_pad(field, axis_num):
    length = field.shape[axis_num]
    head = lax.slice_in_dim(field, length - 4, length, axis=axis_num)
    tail = lax.slice_in_dim(field, 0, 4, axis=axis_num)
    return jnp.concatenate([head, field, tail], axis=axis_num)


def operate(padded_x, field, potential):
    planes = field.shape[1]
    rows_y = field.shape[2]
    cols_z = field.shape[3]
    padded_yz = wrap_pad(wrap_pad(field, 2), 3)
    laplace = 3.0 * lap_weights[0] * field
    for offset in range(1, 5):
        weight = lap_weights[offset]
        along_x = (
            padded_x[:, 4 + offset : 4 + offset + planes]
            + padded_x[:, 4 - offset : 4 - offset + planes]
        )
        along_y = (
            padded_yz[:, :, 4 + offset : 4 + offset + rows_y, 4 : 4 + cols_z]
            + padded_yz[:, :, 4 - offset : 4 - offset + rows_y, 4 : 4 + cols_z]
        )
        along_z = (
            padded_yz[:, :, 4 : 4 + rows_y, 4 + offset : 4 + offset + cols_z]
            + padded_yz[:, :, 4 : 4 + rows_y, 4 - offset : 4 - offset + cols_z]
        )
        laplace = laplace + weight * (along_x + along_y + along_z)
    return potential[None] * field - 0.5 * laplace


def hamiltonian(field, potential):
    padded = padded_2(field, (("grid", 1),), 4)
    return operate(padded, field, potential)


def filter_with(apply_op, start_field, potential):
    center = 0.5 * (upper_edge + lower_edge)
    half_width = 0.5 * (upper_edge - lower_edge)
    prev_field = start_field
    this_field = (apply_op(start_field, potential) - center * start_field) / half_width
    for degree in range(2):
        next_field = (
            2.0 * (apply_op(this_field, potential) - center * this_field) / half_width - prev_field
        )
        prev_field, this_field = (this_field, next_field)
    return this_field


def per_device(orbitals, potential):
    this_field = filter_with(hamiltonian, orbitals, potential)
    local_orbs = orbitals.shape[0]
    field_shape = this_field.shape
    flat_field = this_field.reshape(local_orbs, -1)
    total_cells = float(flat_field.shape[1] * lax.axis_size("grid"))
    contract = (((1,), (1,)), ((), ()))
    highest = lax.Precision.HIGHEST
    gathered = lax.all_gather(flat_field, "orb", axis=0, tiled=True)
    partial_rows = lax.dot_general(flat_field, gathered, contract, precision=highest)
    summed_rows = lax.psum(partial_rows, "grid")
    margin = lax.all_gather(summed_rows, "orb", axis=0, tiled=True) / total_cells
    factor = jnp.linalg.cholesky(margin)
    identity = jnp.eye(margin.shape[0], dtype=jnp.float32)
    inverse = jax.scipy.linalg.solve_triangular(factor, identity, lower=True)
    first_row = lax.axis_index("orb") * local_orbs
    own_rows = lax.dynamic_slice_in_dim(inverse, first_row, local_orbs, 0)
    rotated = jnp.dot(own_rows, gathered, precision=highest)
    return rotated.reshape(field_shape)


def solution(mesh):
    in_specs = (P("orb", "grid", None, None), P("grid", None, None))
    out_specs = P("orb", "grid", None, None)
    return jax.shard_map(
        per_device, mesh=mesh, in_specs=in_specs, out_specs=out_specs, check_vma=False
    )
```

profile of v0, /device:TPU:1, one launch (start us, length us, event | category | flops | bytes accessed | tf_op | source)
XLA Modules:
  0.0 778.8 jit_solution(14914901883185426809)
XLA Ops:
  6.5 2.5 collective-permute-start.1
  9.0 4.7 collective-permute-start
  13.7 2.0 fusion.150
  17.0 5.1 pad_maximum_fusion
  22.1 13.3 %collective-permute-done.1 = f32[64,4,8,128]{3,2,1,0:T(8,128)S(1)} collective-permute-done((f32[64,4,8,128]{3,2,1,0:T(8,128)}, f32[64,4,8,128]{3,2,1,0:T(8,128)S(1)}, u32[]{:S(2)}, u32[]{:S(2)}) %collective-permute-start.1) | collective-permute-done | bytes 1048608 | tf_op jit(solution)/shard_map/ppermute | solution.py:18
  36.4 18.7 %collective-permute-done = f32[64,4,8,128]{3,2,1,0:T(8,128)S(1)} collective-permute-done((f32[64,4,8,128]{3,2,1,0:T(8,128)}, f32[64,4,8,128]{3,2,1,0:T(8,128)S(1)}, u32[]{:S(2)}, u32[]{:S(2)}) %collective-permute-start) | collective-permute-done | bytes 1048608 | tf_op jit(solution)/shard_map/ppermute | solution.py:20
  56.8 16.4 %broadcast_multiply_fusion.1 = (f32[64,4,8,128]{3,2,1,0:T(8,128)S(1)}, f32[64,4,8,128]{3,2,1,0:T(8,128)}) fusion(f32[64,4,8,128]{3,2,1,0:T(8,128)S(1)} %copy-done, f32[64,4,16,132]{3,2,1,0:T(8,128)} %get-tuple-element.34, f32[64,4,16,132]{3,2,1,0:T(8,128)} %get-tuple-element.33, f32[64,4,4,128]{3,2,1,0:T(4,128)S(1)} %get-tuple-element.43, ...), kind=kLoop, calls=%fused_computation.221 | loop fusion | flops 11272192 | bytes 20987904 | tf_op jit(solution)/shard_map/div | solution.py:67
  73.2 4.9 collective-permute-start.2
  79.7 5.1 pad_maximum_fusion.1
  84.9 14.2 %collective-permute-done.2 = f32[64,4,8,128]{3,2,1,0:T(8,128)S(1)} collective-permute-done((f32[64,4,8,128]{3,2,1,0:T(8,128)S(1)}, f32[64,4,8,128]{3,2,1,0:T(8,128)S(1)}, u32[]{:S(2)}, u32[]{:S(2)}) %collective-permute-start.2) | collective-permute-done | bytes 1048608 | tf_op jit(solution)/shard_map/ppermute | solution.py:20
  99.0 22.7 %collective-permute-done.3 = f32[64,4,8,128]{3,2,1,0:T(8,128)S(1)} collective-permute-done((f32[64,4,8,128]{3,2,1,0:T(8,128)S(1)}, f32[64,4,8,128]{3,2,1,0:T(8,128)S(1)}, u32[]{:S(2)}, u32[]{:S(2)}) %collective-permute-start.3) | collective-permute-done | bytes 1048608 | tf_op jit(solution)/shard_map/ppermute | solution.py:18
  122.8 18.3 %fusion.33 = f32[64,4,8,128]{3,2,1,0:T(8,128)S(1)} fusion(f32[64,4,8,128]{3,2,1,0:T(8,128)S(1)} %copy-done, f32[64,4,8,128]{3,2,1,0:T(8,128)} %copy-done.13, f32[64,4,8,128]{3,2,1,0:T(8,128)S(1)} %get-tuple-element.21, f32[64,4,8,128]{3,2,1,0:T(8,128)} %copy-done.11, f32[64,4,4,128]{3,2,1,0:T(4,128)} %copy-done.3, f32[64,4,4,128]{3,2,1,0:T(4,128)} %copy-done.2, ...), kind=kLoop, calls=%fused_computation.106 | loop fusion | flops 13107200 | bytes 15745024 | tf_op jit(solution)/shard_map/sub | solution.py:70
  141.1 3.4 collective-permute-start.4
  146.3 5.1 pad_maximum_fusion.2
  151.4 13.0 %collective-permute-done.4 = f32[64,4,8,128]{3,2,1,0:T(8,128)S(1)} collective-permute-done((f32[64,4,8,128]{3,2,1,0:T(8,128)S(1)}, f32[64,4,8,128]{3,2,1,0:T(8,128)S(1)}, u32[]{:S(2)}, u32[]{:S(2)}) %collective-permute-start.4) | collective-permute-done | bytes 1048608 | tf_op jit(solution)/shard_map/ppermute | solution.py:20
  164.5 23.6 %collective-permute-done.5 = f32[64,4,8,128]{3,2,1,0:T(8,128)S(1)} collective-permute-done((f32[64,4,8,128]{3,2,1,0:T(8,128)S(1)}, f32[64,4,8,128]{3,2,1,0:T(8,128)S(1)}, u32[]{:S(2)}, u32[]{:S(2)}) %collective-permute-start.5) | collective-permute-done | bytes 1048608 | tf_op jit(solution)/shard_map/ppermute | solution.py:18
  189.1 18.1 %fusion.12 = f32[64,4,8,128]{3,2,1,0:T(8,128)S(1)} fusion(f32[64,4,8,128]{3,2,1,0:T(8,128)} %copy-done.14, f32[64,4,8,128]{3,2,1,0:T(8,128)S(1)} %fusion.33, f32[64,4,8,128]{3,2,1,0:T(8,128)} %copy-done.12, f32[64,4,4,128]{3,2,1,0:T(4,128)} %copy-done.5, f32[64,4,4,128]{3,2,1,0:T(4,128)} %copy-done.4, f32[64,4,16,132]{3,2,1,0:T(8,128)} %get-tuple-element.26, ...), kind=kLoop, calls=%fused_computation.85 | loop fusion | flops 13369344 | bytes 14696448 | tf_op jit(solution)/shard_map/sub | solution.py:70
  208.8 80.3 %all-gather.3.cloned.1.call-done = f32[512,4096]{1,0:T(8,128)} async-done(((f32[64,4096]{1,0:T(8,128)}), f32[512,4096]{1,0:T(8,128)}) %all-gather.3.cloned.1.call-update) | async-done | bytes 8388624 | tf_op jit(solution)/shard_map/all_gather | solution.py:84
  289.1 11.3 %fusion.142 = f32[64,512]{1,0:T(8,128)} fusion(f32[512,4096]{1,0:T(8,128)} %all-gather.3.cloned.1.call-done, f32[8,8,32,128]{3,2,1,0:T(8,128)S(1)} %bitcast.61), kind=kOutput, calls=%fused_computation.276 | convolution fusion | flops 1610612736 | bytes 9568256 | tf_op jit(solution)/shard_map/dot_general | solution.py:85
  300.6 276.3 %all-reduce.3.cloned.1.call-done = f32[64,512]{1,0:T(8,128)} async-done(((f32[64,512]{1,0:T(8,128)}), f32[64,512]{1,0:T(8,128)}) %all-reduce.3.cloned.1.call-update) | async-done | bytes 131088 | tf_op jit(solution)/shard_map/psum | solution.py:86
  578.2 41.9 %all-gather.5.cloned.1.call-done = f32[512,512]{1,0:T(8,128)} async-done(((f32[64,512]{1,0:T(8,128)}), f32[512,512]{1,0:T(8,128)}) %all-gather.5.cloned.1.call-update) | async-done | bytes 1048592 | tf_op jit(solution)/shard_map/all_gather | solution.py:87
  622.3 11.7 %cholesky.104 = f32[128,128]{1,0:T(8,128)S(1)} custom-call(f32[128,128]{1,0:T(8,128)S(1)} %cholesky.266), custom_call_target="Cholesky" | custom-call | tf_op jit(solution)/shard_map/jit(cholesky)/cholesky | solution.py:88
  634.2 9.8 %custom-call.31 = f32[1,128,128]{1,2,0:T(8,128)S(1)} custom-call(f32[1,128,128]{2,1,0:T(8,128)S(1)} %get-tuple-element.54), custom_call_target="InvertDiagBlocksLowerTriangular" | custom-call | tf_op jit(solution)/shard_map/jit(cholesky)/cholesky | solution.py:88
  644.7 11.7 %cholesky.217 = f32[128,128]{1,0:T(8,128)S(1)} custom-call(f32[128,128]{1,0:T(8,128)S(1)} %cholesky.270), custom_call_target="Cholesky" | custom-call | tf_op jit(solution)/shard_map/jit(cholesky)/cholesky | solution.py:88
  656.4 10.0 %custom-call.32 = f32[1,128,128]{1,2,0:T(8,128)S(1)} custom-call(f32[1,128,128]{2,1,0:T(8,128)S(1)} %get-tuple-element.51), custom_call_target="InvertDiagBlocksLowerTriangular" | custom-call | tf_op jit(solution)/shard_map/jit(cholesky)/cholesky | solution.py:88
  667.1 12.3 %cholesky.238 = f32[128,128]{1,0:T(8,128)} custom-call(f32[128,128]{1,0:T(8,128)S(1)} %cholesky.275), custom_call_target="Cholesky" | custom-call | tf_op jit(solution)/shard_map/jit(cholesky)/cholesky | solution.py:88
  681.6 11.3 %custom-call.33 = f32[1,128,128]{1,2,0:T(8,128)} custom-call(f32[1,128,128]{2,1,0:T(8,128)} %get-tuple-element.48), custom_call_target="InvertDiagBlocksLowerTriangular" | custom-call | tf_op jit(solution)/shard_map/jit(cholesky)/cholesky | solution.py:88
  694.3 11.9 %cholesky.255 = f32[128,128]{1,0:T(8,128)S(1)} custom-call(f32[128,128]{1,0:T(8,128)S(1)} %convolution_subtract_fusion.5), custom_call_target="Cholesky" | custom-call | tf_op jit(solution)/shard_map/jit(cholesky)/cholesky | solution.py:88
  710.1 9.9 %while.1 = (s32[]{:T(128)}, f32[512,512]{1,0:T(8,128)S(1)}, s32[4,2]{0,1:T(2,128)S(1)}, f32[4,128,128]{2,1,0:T(8,128)}, s32[]{:T(128)}) while((s32[]{:T(128)}, f32[512,512]{1,0:T(8,128)S(1)}, s32[4,2]{0,1:T(2,128)S(1)}, f32[4,128,128]{2,1,0:T(8,128)}, s32[]{:T(128)}) %tuple.38), condition=%wide.while_cond, body=%wide.while_body.sunk | while | flops 2 | bytes 132705 | solution.py:90
  713.2 1.9 bitcast_dynamic-update-slice_fusion.2
  720.0 40.1 %custom-call.34 = f32[4,128,128]{1,2,0:T(8,128)S(1)} custom-call(f32[4,128,128]{2,1,0:T(8,128)} %get-tuple-element.12), custom_call_target="InvertDiagBlocksLowerTriangular" | custom-call | tf_op jit(solution)/shard_map/jit(_solve_triangular)/triangular_solve | solution.py:90
  763.2 7.5 convolution_bitcast_fusion
  (99 shorter events, 33.4 us)
Async XLA Ops:
  6.5 9.2 %copy-start = (f32[64,4,8,128]{3,2,1,0:T(8,128)S(1)}, f32[64,4,8,128]{3,2,1,0:T(8,128)}, u32[]{:S(2)}) copy-start(f32[64,4,8,128]{3,2,1,0:T(8,128)} %param.2) | copy-start | bytes 3145732
  6.5 9.2 %copy-start.15 = (f32[4,8,128]{2,1,0:T(8,128)S(1)}, f32[4,8,128]{2,1,0:T(8,128)}, u32[]{:S(2)}) copy-start(f32[4,8,128]{2,1,0:T(8,128)} %param.3) | copy-start | bytes 49156
  6.5 282.6 %all-gather.3.cloned.1.call-start = ((), (), s32[]{:S(2)}) async-start(), calls=%async_computation | async-start | bytes 9437184 | tf_op jit(solution)/shard_map/all_gather | solution.py:84
  6.5 28.8 %collective-permute-start.1 = (f32[64,4,8,128]{3,2,1,0:T(8,128)}, f32[64,4,8,128]{3,2,1,0:T(8,128)S(1)}, u32[]{:S(2)}, u32[]{:S(2)}) collective-permute-start(f32[64,4,8,128]{3,2,1,0:T(8,128)} %param.2), channel_id=1, source_target_pairs={{0,8},{8,16},{16,24},{24,32},{32,40},{40,48},{48,56},{56,64},{64,7... | collective-permute-start | bytes 3145736 | tf_op jit(solution)/shard_map/ppermute | solution.py:18
  9.0 46.1 %collective-permute-start = (f32[64,4,8,128]{3,2,1,0:T(8,128)}, f32[64,4,8,128]{3,2,1,0:T(8,128)S(1)}, u32[]{:S(2)}, u32[]{:S(2)}) collective-permute-start(f32[64,4,8,128]{3,2,1,0:T(8,128)} %param.2), channel_id=1, source_target_pairs={{8,0},{16,8},{24,16},{32,24},{40,32},{48,40},{56,48},{64,56},{72,6... | collective-permute-start | bytes 3145736 | tf_op jit(solution)/shard_map/ppermute | solution.py:20
  35.4 1.0 copy-start.8
  36.4 18.8 %copy-start.7 = (f32[64,8,8,128]{3,2,1,0:T(8,128)}, f32[64,8,8,128]{3,2,1,0:T(8,128)S(1)}, u32[]{:S(2)}) copy-start(f32[64,8,8,128]{3,2,1,0:T(8,128)S(1)} %get-tuple-element.42) | copy-start | bytes 6291460
  55.1 1.0 copy-start.9
  55.2 1.6 copy-start.6
  73.2 25.8 %collective-permute-start.2 = (f32[64,4,8,128]{3,2,1,0:T(8,128)S(1)}, f32[64,4,8,128]{3,2,1,0:T(8,128)S(1)}, u32[]{:S(2)}, u32[]{:S(2)}) collective-permute-start(f32[64,4,8,128]{3,2,1,0:T(8,128)S(1)} %get-tuple-element.21), channel_id=1, source_target_pairs={{8,0},{16,8},{24,16},{32,24},{40,32},{48,40},{56,48},{64,56},{72,6... | collective-permute-start | bytes 3145736 | tf_op jit(solution)/shard_map/ppermute | solution.py:20
  78.1 43.6 %collective-permute-start.3 = (f32[64,4,8,128]{3,2,1,0:T(8,128)S(1)}, f32[64,4,8,128]{3,2,1,0:T(8,128)S(1)}, u32[]{:S(2)}, u32[]{:S(2)}) collective-permute-start(f32[64,4,8,128]{3,2,1,0:T(8,128)S(1)} %get-tuple-element.21), channel_id=1, source_target_pairs={{0,8},{8,16},{16,24},{24,32},{32,40},{40,48},{48,56},{56,64},{64,7... | collective-permute-start | bytes 3145736 | tf_op jit(solution)/shard_map/ppermute | solution.py:18
  78.5 1.3 copy-start.2
  78.5 1.3 copy-start.3
  99.0 22.7 %copy-start.11 = (f32[64,4,8,128]{3,2,1,0:T(8,128)}, f32[64,4,8,128]{3,2,1,0:T(8,128)S(1)}, u32[]{:S(2)}) copy-start(f32[64,4,8,128]{3,2,1,0:T(8,128)S(1)} %collective-permute-done.2) | copy-start | bytes 3145732
  121.7 1.1 copy-start.13
  141.1 23.3 %collective-permute-start.4 = (f32[64,4,8,128]{3,2,1,0:T(8,128)S(1)}, f32[64,4,8,128]{3,2,1,0:T(8,128)S(1)}, u32[]{:S(2)}, u32[]{:S(2)}) collective-permute-start(f32[64,4,8,128]{3,2,1,0:T(8,128)S(1)} %fusion.33), channel_id=1, source_target_pairs={{8,0},{16,8},{24,16},{32,24},{40,32},{48,40},{56,48},{64,56},{72,6... | collective-permute-start | bytes 3145736 | tf_op jit(solution)/shard_map/ppermute | solution.py:20
  144.5 43.5 %collective-permute-start.5 = (f32[64,4,8,128]{3,2,1,0:T(8,128)S(1)}, f32[64,4,8,128]{3,2,1,0:T(8,128)S(1)}, u32[]{:S(2)}, u32[]{:S(2)}) collective-permute-start(f32[64,4,8,128]{3,2,1,0:T(8,128)S(1)} %fusion.33), channel_id=1, source_target_pairs={{0,8},{8,16},{16,24},{24,32},{32,40},{40,48},{48,56},{56,64},{64,7... | collective-permute-start | bytes 3145736 | tf_op jit(solution)/shard_map/ppermute | solution.py:18
  145.1 1.3 copy-start.4
  145.1 1.3 copy-start.5
  146.3 42.8 %copy-start.1 = (f32[64,4,8,128]{3,2,1,0:T(8,128)S(1)}, f32[64,4,8,128]{3,2,1,0:T(8,128)}, u32[]{:S(2)}) copy-start(f32[64,4,8,128]{3,2,1,0:T(8,128)} %get-tuple-element.22) | copy-start | bytes 3145732
  164.5 23.6 %copy-start.12 = (f32[64,4,8,128]{3,2,1,0:T(8,128)}, f32[64,4,8,128]{3,2,1,0:T(8,128)S(1)}, u32[]{:S(2)}) copy-start(f32[64,4,8,128]{3,2,1,0:T(8,128)S(1)} %collective-permute-done.4) | copy-start | bytes 3145732
  188.0 1.1 copy-start.14
  208.8 368.2 %all-reduce.3.cloned.1.call-start = ((), (), s32[]{:S(2)}) async-start(), calls=%async_computation.1 | async-start | bytes 262144 | tf_op jit(solution)/shard_map/psum | solution.py:86
  300.4 319.7 %all-gather.5.cloned.1.call-start = ((), (), s32[]{:S(2)}) async-start(), calls=%async_computation.2 | async-start | bytes 1179648 | tf_op jit(solution)/shard_map/all_gather | solution.py:87
  679.4 81.0 %copy-start.10 = (f32[512,512]{1,0:T(8,128)S(1)}, f32[512,512]{1,0:T(8,128)}, u32[]{:S(2)}) copy-start(f32[512,512]{1,0:T(8,128)} %fusion.114) | copy-start | bytes 3145732
Sparse Core Ops, SparseCore 0:
  208.9 80.1 all-gather.2
  300.5 276.3 all-reduce.2
  579.0 41.0 all-gather.4
where the time goes:
time: 786 us; the launch traced here: 779 us
  waiting for transfers between devices  504 us (64%)
  other arithmetic  193 us (25%)
  matrix products  24.5 us (3%)
  local copies, waits for them, and re-layouts  24.2 us (3%)
  between operations  16.5 us (2%)
  starting transfers between devices  16.3 us (2%)
    psum x1, waiting for transfers between devices, per_device(): summed_rows = lax.psum(partial_rows, 'grid')  276 us
    another operation x14, other arithmetic, per_device(): factor = jnp.linalg.cholesky(margin)  82.3 us
    all_gather x1, waiting for transfers between devices, per_device(): gathered = lax.all_gather(flat_field, 'orb', axis=0, tiled=True)  80.3 us
    ppermute x3, waiting for transfers between devices, padded_2(): lax.ppermute(tail, axis, [(i, (i + 1) % count) for i in range(count)])  59.6 us
    ppermute x3, waiting for transfers between devices, padded_2(): lax.ppermute(head, axis, [((i + 1) % count, i) for i in range(count)])  45.9 us
    all_gather x1, waiting for transfers between devices, per_device(): lax.all_gather(summed_rows, 'orb', axis=0, tiled=True) / total_cells  41.9 us
    another operation x3, other arithmetic, per_device(): inverse = jax.scipy.linalg.solve_triangular(factor, identity, lower=True)  40.3 us
    sub x2, other arithmetic, filter_with(): 2.0 * (apply_op(this_field, potential) - center * this_field) / half_width  36.4 us
  transfers between devices with their start and end apart: 9, of which 9 were waited for; matrix products, arithmetic and copies ran while one was open for 3% of the time, Pallas kernels for 0%

commit v1 on v0

v1 whole, which is shorter than its diff:
```python
import functools
import jax, jax.numpy as jnp
from jax import lax
from jax.sharding import PartitionSpec as P
from jax.experimental import pallas as pl
from jax.experimental.pallas import tpu as pltpu
HI = lax.Precision.HIGHEST
NT = (((1,), (1,)), ((), ()))
NN = (((1,), (0,)), ((), ()))

def dot(a, b, dims):
    return lax.dot_general(a, b, dims, precision=HI, preferred_element_type=jnp.float32)

def row_of(block, j):
    return jnp.broadcast_to(block[j:j + 1, :], (8, 128))

def recip(d):
    r = pl.reciprocal(d, approx=True)
    r = r * (2.0 - d * r)
    return r * (2.0 - d * r)

def factor_block(s_ref, w_ref, base):
    sub = lax.broadcasted_iota(jnp.int32, (8, 128), 0)
    lane = lax.broadcasted_iota(jnp.int32, (8, 128), 1)
    s = [s_ref[pl.ds(base + 8 * i, 8), :] for i in range(16)]
    w = [jnp.where(lane == sub + 8 * i, 1.0, 0.0).astype(jnp.float32) for i in range(16)]
    for p in range(16):
        col = [jnp.broadcast_to(s[p][:, 8 * p + j:8 * p + j + 1], (8, 128)) for j in range(8)]
        fac, rinv, s_rows, w_rows = {}, [], [], []
        sp, wp = s[p], w[p]
        dvec = jnp.ones((8, 128), jnp.float32)
        for j in range(8):
            d = row_of(col[j], j)
            r = recip(d)
            rinv.append(r)
            dvec = jnp.where(sub == j, d, dvec)
            m = jnp.where(sub > j, col[j] * r, 0.0)
            for k in range(j + 1, 8):
                fac[j, k] = row_of(col[k], j)
                col[k] = col[k] - m * fac[j, k]
            s_rows.append(row_of(sp, j))
            w_rows.append(row_of(wp, j))
            if j < 7:
                sp = sp - m * s_rows[j]
                wp = wp - m * w_rows[j]
        w[p] = wp * lax.rsqrt(dvec)
        for i in range(p + 1, 16):
            raw = [jnp.broadcast_to(s[i][:, 8 * p + j:8 * p + j + 1], (8, 128)) for j in range(8)]
            si, wi = s[i], w[i]
            for j in range(8):
                m = raw[j] * rinv[j]
                for k in range(j + 1, 8):
                    raw[k] = raw[k] - m * fac[j, k]
                si = si - m * s_rows[j]
                wi = wi - m * w_rows[j]
            s[i], w[i] = si, wi
    for i in range(16):
        w_ref[8 * i:8 * i + 8, :] = w[i]

def blk(i, j):
    return i * (i + 1) // 2 + j

def rotate_kernel(cells, g_ref, f_ref, y_ref, a_ref, x_ref, w_ref):
    a_ref[...] = g_ref[...] * (1.0 / cells)
    for q in range(4):
        x_ref[:, 128 * q:128 * q + 128] = f_ref[:, q, :]
    for b in range(4):
        factor_block(a_ref, w_ref, 128 * blk(b, b))
        w = w_ref[...]
        low = {}
        for i in range(b + 1, 4):
            low[i] = dot(a_ref[pl.ds(128 * blk(i, b), 128), :], w, NT)
            for j in range(b + 1, i + 1):
                rows = pl.ds(128 * blk(i, j), 128)
                a_ref[rows, :] = a_ref[rows, :] - dot(low[i], low[j], NT)
        y = dot(w, x_ref[128 * b:128 * b + 128, :], NN)
        for q in range(4):
            y_ref[128 * b:128 * b + 128, q, :] = y[:, 128 * q:128 * q + 128]
        for i in range(b + 1, 4):
            rows = slice(128 * i, 128 * i + 128)
            x_ref[rows, :] = x_ref[rows, :] - dot(low[i], y, NN)

def rotate(g, f, cells):
    vm = pl.BlockSpec(memory_space=pltpu.VMEM)
    return pl.pallas_call(functools.partial(rotate_kernel, cells),
        out_shape=jax.ShapeDtypeStruct((512, 4, 128), jnp.float32),
        in_specs=[vm, vm], out_specs=vm,
        scratch_shapes=[pltpu.VMEM((1280, 128), jnp.float32), pltpu.VMEM((512, 512), jnp.float32), pltpu.VMEM((128, 128), jnp.float32)],
        compiler_params=pltpu.CompilerParams(vmem_limit_bytes=32 << 20))(g, f)

def margin_kernel(f_ref, g_ref, x_ref):
    for q in range(4):
        x_ref[:, 128 * q:128 * q + 128] = f_ref[:, q, :]
    for i in range(4):
        xi = x_ref[128 * i:128 * i + 128, :]
        for j in range(i + 1):
            g_ref[pl.ds(128 * blk(i, j), 128), :] = dot(xi, x_ref[128 * j:128 * j + 128, :], NT)

def margin_part(f):
    vm = pl.BlockSpec(memory_space=pltpu.VMEM)
    return pl.pallas_call(margin_kernel, out_shape=jax.ShapeDtypeStruct((1280, 128), jnp.float32),
        in_specs=[vm], out_specs=vm, scratch_shapes=[pltpu.VMEM((512, 512), jnp.float32)],
        compiler_params=pltpu.CompilerParams(vmem_limit_bytes=32 << 20))(f)

W = (-205.0 / 72.0, 8.0 / 5.0, -1.0 / 5.0, 8.0 / 315.0, -1.0 / 560.0)

def filter_kernel(v_ref, p_ref, o_ref, a_ref, b_ref):
    step = 4
    def fill(ref):
        ref[:, 0:4] = ref[:, 128:132]
        ref[:, 132:136] = ref[:, 4:8]
    def level(src, prev, dst, gain):
        scale = -0.5 * gain
        w = [scale * c for c in W]
        def body(t, carry):
            base = t * step
            pot = p_ref[pl.ds(base, step)]
            diag = gain * (pot - 7.0) + 3.0 * w[0]
            for o in range(2):
                win = src[o, pl.ds(base, step + 8)]
                v = win[4:4 + step]
                acc = diag * v
                u1 = pltpu.roll(v, 1, 1) + pltpu.roll(v, 7, 1)
                r4 = pltpu.roll(v, 4, 1)
                u2 = pltpu.roll(v + r4, 2, 1)
                u3 = pltpu.roll(u1, 4, 1)
                side = [u1, u2, u3, r4 + r4]
                for m in range(1, 5):
                    zz = pltpu.roll(v, m, 2) + pltpu.roll(v, 128 - m, 2)
                    xx = win[4 + m:4 + m + step] + win[4 - m:4 - m + step]
                    acc = acc + w[m] * (side[m - 1] + zz + xx)
                if prev is not None:
                    acc = acc - prev(o, base)
                dst(o, base, acc)
            return carry
        lax.fori_loop(0, 128 // step, body, 0)
    a_ref[:, 4:132] = v_ref[...]
    fill(a_ref)
    def into(ref, off):
        def put(o, base, val):
            ref[o, pl.ds(base + off, step)] = val
        return put
    def of(ref, off):
        return lambda o, base: ref[o, pl.ds(base + off, step)]
    level(a_ref, None, into(b_ref, 4), 0.25)
    fill(b_ref)
    level(b_ref, of(a_ref, 4), into(a_ref, 4), 0.5)
    fill(a_ref)
    level(a_ref, of(b_ref, 4), into(o_ref, 0), 0.5)

def filt(v, p):
    vm = pl.BlockSpec(memory_space=pltpu.VMEM)
    return pl.pallas_call(filter_kernel, out_shape=jax.ShapeDtypeStruct(v.shape, jnp.float32),
        in_specs=[vm, vm], out_specs=vm,
        scratch_shapes=[pltpu.VMEM((2, 136, 8, 128), jnp.float32)] * 2,
        compiler_params=pltpu.CompilerParams(vmem_limit_bytes=32 << 20))(v, p)

MESH = pl.DeviceIdType.MESH


def any_spec():
    return pl.BlockSpec(memory_space=pl.ANY)


def spread_kernel(orb_ref, pot_ref, v_ref, p_ref, send, recv, psend, precv, own):
    me, my_orb = lax.axis_index("grid"), lax.axis_index("orb")
    bar = pltpu.get_barrier_semaphore()

    def greet(d, carry):
        pl.semaphore_signal(bar, inc=1, device_id=(lax.rem(me + d, 32), my_orb), device_id_type=MESH)
        return carry

    lax.fori_loop(1, 32, greet, 0)
    pl.semaphore_wait(bar, 31)

    def copies(d):
        to = lax.rem(me + d, 32)
        field = pltpu.make_async_remote_copy(
            src_ref=orb_ref.at[pl.ds(2 * to, 2)],
            dst_ref=v_ref.at[:, pl.ds(4 * me, 4)],
            send_sem=send.at[d], recv_sem=recv.at[d],
            device_id=(to, my_orb), device_id_type=MESH)
        pot = pltpu.make_async_remote_copy(
            src_ref=pot_ref, dst_ref=p_ref.at[pl.ds(4 * me, 4)],
            send_sem=psend.at[d], recv_sem=precv.at[d],
            device_id=(to, my_orb), device_id_type=MESH)
        return field, pot

    def start(d, carry):
        for c in copies(d):
            c.start()
        return carry

    lax.fori_loop(1, 32, start, 0)
    mine = pltpu.make_async_copy(orb_ref.at[pl.ds(2 * me, 2)], v_ref.at[:, pl.ds(4 * me, 4)], own.at[0])
    mine.start()
    minep = pltpu.make_async_copy(pot_ref, p_ref.at[pl.ds(4 * me, 4)], own.at[1])
    minep.start()
    mine.wait()
    minep.wait()

    def finish(d, carry):
        for c in copies(d):
            c.wait()
        return carry

    lax.fori_loop(1, 32, finish, 0)


def spread(orbitals, potential):
    dma = pltpu.SemaphoreType.DMA
    return pl.pallas_call(
        spread_kernel,
        out_shape=(jax.ShapeDtypeStruct((2, 128, 8, 128), jnp.float32),
                   jax.ShapeDtypeStruct((128, 8, 128), jnp.float32)),
        in_specs=[any_spec()] * 2, out_specs=(any_spec(),) * 2,
        scratch_shapes=[dma((32,))] * 4 + [dma((2,))],
        compiler_params=pltpu.CompilerParams(collective_id=1, has_side_effects=True),
    )(orbitals, potential)


def collect_kernel(f_ref, m_ref, slab, send, recv, send2, recv2, own):
    me, my_orb = lax.axis_index("grid"), lax.axis_index("orb")
    bar = pltpu.get_barrier_semaphore()

    def greet(d, carry):
        pl.semaphore_signal(bar, inc=1, device_id=(lax.rem(me + d, 32), my_orb), device_id_type=MESH)
        return carry

    def greet_orb(d, carry):
        pl.semaphore_signal(bar, inc=1, device_id=(me, lax.rem(my_orb + d, 8)), device_id_type=MESH)
        return carry

    lax.fori_loop(1, 32, greet, 0)
    lax.fori_loop(1, 8, greet_orb, 0)
    pl.semaphore_wait(bar, 38)

    def piece(d):
        to = lax.rem(me + d, 32)
        return pltpu.make_async_remote_copy(
            src_ref=f_ref.at[:, pl.ds(4 * to, 4)],
            dst_ref=slab.at[pl.ds(2 * me, 2)],
            send_sem=send.at[d], recv_sem=recv.at[d],
            device_id=(to, my_orb), device_id_type=MESH)

    def start(d, carry):
        piece(d).start()
        return carry

    lax.fori_loop(1, 32, start, 0)
    mine = pltpu.make_async_copy(f_ref.at[:, pl.ds(4 * me, 4)], slab.at[pl.ds(2 * me, 2)], own.at[0])
    mine.start()
    mine.wait()

    def finish(d, carry):
        piece(d).wait()
        return carry

    lax.fori_loop(1, 32, finish, 0)

    def cells(d):
        to = lax.rem(my_orb + d, 8)
        return pltpu.make_async_remote_copy(
            src_ref=slab.at[:, to // 2, lax.rem(to, 2)],
            dst_ref=m_ref.at[pl.ds(64 * my_orb, 64)],
            send_sem=send2.at[d], recv_sem=recv2.at[d],
            device_id=(me, to), device_id_type=MESH)

    for d in range(1, 8):
        cells(d).start()
    mine = pltpu.make_async_copy(slab.at[:, my_orb // 2, lax.rem(my_orb, 2)], m_ref.at[pl.ds(64 * my_orb, 64)], own.at[1])
    mine.start()
    mine.wait()
    for d in range(1, 8):
        cells(d).wait()


def collect(f):
    dma = pltpu.SemaphoreType.DMA
    return pl.pallas_call(
        collect_kernel,
        out_shape=jax.ShapeDtypeStruct((512, 4, 128), jnp.float32),
        in_specs=[any_spec()], out_specs=any_spec(),
        scratch_shapes=[pltpu.VMEM((64, 4, 2, 4, 128), jnp.float32), dma((32,)), dma((32,)), dma((8,)), dma((8,)), dma((2,))],
        compiler_params=pltpu.CompilerParams(collective_id=2, has_side_effects=True, vmem_limit_bytes=32 << 20),
    )(f)


def reduce_kernel(g_ref, out_ref, parts, zparts, send, recv, zsend, zrecv, asend, arecv, own):
    me, my_orb = lax.axis_index("grid"), lax.axis_index("orb")
    z_lo, z_hi = lax.rem(me, 2), my_orb // 2
    at = (me // 2) * 2 + lax.rem(my_orb, 2)
    zat = z_hi * 2 + z_lo

    def plane(i):
        return (i // 2) * 2 + z_lo, z_hi * 2 + lax.rem(i, 2)

    def column(z):
        return (me // 2) * 2 + lax.rem(z, 2), (z // 2) * 2 + lax.rem(my_orb, 2)

    bar = pltpu.get_barrier_semaphore()

    def greet(d, carry):
        pl.semaphore_signal(bar, inc=1, device_id=plane(lax.rem(at + d, 32)), device_id_type=MESH)
        return carry

    def greet_z(d, carry):
        pl.semaphore_signal(bar, inc=1, device_id=column(lax.rem(zat + d, 8)), device_id_type=MESH)
        return carry

    lax.fori_loop(1, 32, greet, 0)
    lax.fori_loop(1, 8, greet_z, 0)
    pl.semaphore_wait(bar, 38)

    def scatter(d):
        to = lax.rem(at + d, 32)
        return pltpu.make_async_remote_copy(
            src_ref=g_ref.at[pl.ds(pl.multiple_of(40 * to, 8), 40)], dst_ref=parts.at[at],
            send_sem=send.at[d], recv_sem=recv.at[d],
            device_id=plane(to), device_id_type=MESH)

    def start(d, carry):
        scatter(d).start()
        return carry

    lax.fori_loop(1, 32, start, 0)
    my_rows = pl.ds(pl.multiple_of(40 * at, 8), 40)
    parts[at] = g_ref[my_rows, :]

    def finish(d, carry):
        scatter(d).wait()
        return carry

    lax.fori_loop(1, 32, finish, 0)

    def add(i, total):
        return total + parts[i]

    zparts[zat] = lax.fori_loop(1, 32, add, parts[0])

    def exchange(d):
        return pltpu.make_async_remote_copy(
            src_ref=zparts.at[zat], dst_ref=zparts.at[zat],
            send_sem=zsend.at[d], recv_sem=zrecv.at[d],
            device_id=column(lax.rem(zat + d, 8)), device_id_type=MESH)

    for d in range(1, 8):
        exchange(d).start()
    for d in range(1, 8):
        exchange(d).wait()
    total = zparts[0]
    for z in range(1, 8):
        total = total + zparts[z]
    out_ref[my_rows, :] = total

    def gather(d):
        return pltpu.make_async_remote_copy(
            src_ref=out_ref.at[my_rows], dst_ref=out_ref.at[my_rows],
            send_sem=asend.at[d], recv_sem=arecv.at[d],
            device_id=plane(lax.rem(at + d, 32)), device_id_type=MESH)

    def start3(d, carry):
        gather(d).start()
        return carry

    def finish3(d, carry):
        gather(d).wait()
        return carry

    lax.fori_loop(1, 32, start3, 0)
    lax.fori_loop(1, 32, finish3, 0)


def reduce_all(g):
    dma = pltpu.SemaphoreType.DMA
    vm = pl.BlockSpec(memory_space=pltpu.VMEM)
    return pl.pallas_call(
        reduce_kernel,
        out_shape=jax.ShapeDtypeStruct((1280, 128), jnp.float32),
        in_specs=[vm], out_specs=vm,
        scratch_shapes=[pltpu.VMEM((32, 40, 128), jnp.float32), pltpu.VMEM((8, 40, 128), jnp.float32),
                        dma((32,)), dma((32,)), dma((8,)), dma((8,)), dma((32,)), dma((32,)), dma((2,))],
        compiler_params=pltpu.CompilerParams(collective_id=3, has_side_effects=True, vmem_limit_bytes=32 << 20),
    )(g)


def deliver_kernel(y_ref, out_ref, send, recv, own):
    me, my_orb = lax.axis_index("grid"), lax.axis_index("orb")
    bar = pltpu.get_barrier_semaphore()
    for d in range(1, 8):
        pl.semaphore_signal(bar, inc=1, device_id=(me, lax.rem(my_orb + d, 8)), device_id_type=MESH)
    pl.semaphore_wait(bar, 7)

    def rows(d):
        to = lax.rem(my_orb + d, 8)
        return pltpu.make_async_remote_copy(
            src_ref=y_ref.at[pl.ds(64 * to, 64)],
            dst_ref=out_ref.at[:, my_orb // 2, lax.rem(my_orb, 2)],
            send_sem=send.at[d], recv_sem=recv.at[d],
            device_id=(me, to), device_id_type=MESH)

    for d in range(1, 8):
        rows(d).start()
    mine = pltpu.make_async_copy(y_ref.at[pl.ds(64 * my_orb, 64)], out_ref.at[:, my_orb // 2, lax.rem(my_orb, 2)], own.at[0])
    mine.start()
    mine.wait()
    for d in range(1, 8):
        rows(d).wait()


def deliver(y):
    dma = pltpu.SemaphoreType.DMA
    return pl.pallas_call(
        deliver_kernel,
        out_shape=jax.ShapeDtypeStruct((64, 4, 2, 4, 128), jnp.float32),
        in_specs=[any_spec()], out_specs=any_spec(),
        scratch_shapes=[dma((8,)), dma((8,)), dma((1,))],
        compiler_params=pltpu.CompilerParams(collective_id=4, has_side_effects=True),
    )(y)


def per_device(orbitals, potential):
    field, pot = spread(orbitals, potential)
    filtered = filt(field, pot)
    cells = collect(filtered.reshape(2, 128, 2, 4, 128))
    margin = reduce_all(margin_part(cells))
    rotated = rotate(margin, cells, 131072.0)
    return deliver(rotated).reshape(64, 4, 8, 128)


def solution(mesh):
    in_specs = (P("orb", "grid", None, None), P("grid", None, None))
    out_specs = P("orb", "grid", None, None)
    return jax.shard_map(
        per_device, mesh=mesh, in_specs=in_specs, out_specs=out_specs, check_vma=False
    )
```

time: 786 us -> 185 us (0.24)
  waiting for transfers between devices: 504 us -> 0 us
  other arithmetic: 193 us -> 0 us
  Pallas kernels: 0 us -> 178 us
  matrix products: 24.5 us -> 0 us
  local copies, waits for them, and re-layouts: 24.2 us -> 5.49 us
  between operations: 16.5 us -> 0.07 us
  starting transfers between devices: 16.3 us -> 0 us
    psum x1 -> x0, waiting for transfers between devices: 276 us -> none  [per_device(): summed_rows = lax.psum(partial_rows, 'grid')]
    pallas_call x0 -> x7, Pallas kernels: none -> 178 us  [the longest x1 48.8 us: collect(): pl.pallas_call(collect_kernel, out_shape=jax.ShapeDtypeStruct((512, 4, 12...]
    another operation x17 -> x0, other arithmetic: 123 us -> none  [the longest x14 82.3 us: per_device(): factor = jnp.linalg.cholesky(margin)]
    all_gather x2 -> x0, waiting for transfers between devices: 122 us -> none  [the longest x1 80.3 us: per_device(): gathered = lax.all_gather(flat_field, 'orb', axis=0, tiled=True)]
    ppermute x6 -> x0, waiting for transfers between devices: 105 us -> none  [the longest x3 59.6 us: padded_2(): lax.ppermute(tail, axis, [(i, (i + 1) % count) for i in range(count)])]
    sub x2 -> x0, other arithmetic: 36.4 us -> none  [filter_with(): 2.0 * (apply_op(this_field, potential) - center * this_field) / half_width]
    dot_general x2 -> x0, matrix products: 18.8 us -> none  [the longest x1 11.3 us: per_device(): lax.dot_general(flat_field, gathered, contract, precision=highest)]
    div x3 -> x0, other arithmetic: 16.7 us -> none  [the longest x1 16.4 us: filter_with(): (apply_op(start_field, potential) - center * start_field) / half_width]
  transfers between devices with their start and end apart: 9 -> 0, of which waited for: 9 -> 0; matrix products, arithmetic and copies ran while one was open for 3% -> 0% of each run, Pallas kernels for 0% -> 0%
where the time goes in v1:
time: 185 us; the launch traced here: 184 us
  Pallas kernels  178 us (96%)
  local copies, waits for them, and re-layouts  5.49 us (3%)
    pallas_call x1, Pallas kernels, collect(): pl.pallas_call(collect_kernel, out_shape=jax.ShapeDtypeStruct((512, 4, 12...  48.8 us
    pallas_call x1, Pallas kernels, reduce_all(): pl.pallas_call(reduce_kernel, out_shape=jax.ShapeDtypeStruct((1280, 128),...  33.9 us
    pallas_call x1, Pallas kernels, spread(): pl.pallas_call(spread_kernel, out_shape=(jax.ShapeDtypeStruct((2, 128, 8,...  28.5 us
    pallas_call x1, Pallas kernels, deliver(): pl.pallas_call(deliver_kernel, out_shape=jax.ShapeDtypeStruct((64, 4, 2,...  27.9 us
    pallas_call x1, Pallas kernels, rotate(): pl.pallas_call(functools.partial(rotate_kernel, cells), out_shape=jax.Sha...  23.2 us
    pallas_call x1, Pallas kernels, filt(): pl.pallas_call(filter_kernel, out_shape=jax.ShapeDtypeStruct(v.shape, jnp...  13.5 us
    unnamed x7, local copies, waits for them, and re-layouts  5.49 us

profile of v1, /device:TPU:1, one launch (start us, length us, event | category | flops | bytes accessed | tf_op | source)
XLA Modules:
  0.0 183.7 jit_solution(12259064953283246135)
XLA Ops:
  0.0 28.5 %shard_map.28 = (f32[2,128,8,128]{3,2,1,0:T(8,128)}, f32[128,8,128]{2,1,0:T(8,128)}) custom-call(f32[64,4,8,128]{3,2,1,0:T(8,128)} %orb_ref.1, f32[4,8,128]{2,1,0:T(8,128)} %pot_ref.1), custom_call_target="tpu_custom_call" | custom-call | tf_op jit(solution)/shard_map/pallas_call | solution.py:212
  28.5 0.0 copy-start.1
  28.5 1.2 copy-done.1
  29.7 0.0 copy-start.2
  29.7 1.0 copy-done.2
  30.7 13.5 %shard_map.29 = f32[2,128,8,128]{3,2,1,0:T(8,128)S(1)} custom-call(f32[2,128,8,128]{3,2,1,0:T(8,128)S(1)} %copy-done.1, f32[128,8,128]{2,1,0:T(8,128)S(1)} %copy-done.2), custom_call_target="tpu_custom_call" | custom-call | tf_op jit(solution)/shard_map/pallas_call | solution.py:153
  44.3 48.8 %shard_map.30.f_ref = f32[512,4,128]{2,1,0:T(4,128)S(1)} custom-call(f32[2,128,2,4,128]{4,3,2,1,0:T(4,128)S(1)} %bitcast.2), custom_call_target="tpu_custom_call" | custom-call | tf_op jit(solution)/shard_map/pallas_call | solution.py:280
  93.1 2.4 %shard_map.31.g_ref = f32[1280,128]{1,0:T(8,128)S(1)} custom-call(f32[512,4,128]{2,1,0:T(4,128)S(1)} %shard_map.30.f_ref), custom_call_target="tpu_custom_call" | custom-call | tf_op jit(solution)/shard_map/pallas_call | solution.py:101
  95.5 33.9 %shard_map.32.g_ref = f32[1280,128]{1,0:T(8,128)S(1)} custom-call(f32[1280,128]{1,0:T(8,128)S(1)} %shard_map.31.g_ref), custom_call_target="tpu_custom_call" | custom-call | tf_op jit(solution)/shard_map/pallas_call | solution.py:377
  129.4 23.2 %shard_map.33.y_ref = f32[512,4,128]{2,1,0:T(4,128)S(1)} custom-call(f32[1280,128]{1,0:T(8,128)S(1)} %shard_map.32.g_ref, f32[512,4,128]{2,1,0:T(4,128)S(1)} %shard_map.30.f_ref), custom_call_target="tpu_custom_call" | custom-call | tf_op jit(solution)/shard_map/pallas_call | solution.py:85
  152.6 0.0 copy-start
  152.6 1.0 copy-done
  153.6 27.9 %shard_map.34 = f32[64,4,2,4,128]{4,3,2,1,0:T(4,128)} custom-call(f32[512,4,128]{2,1,0:T(4,128)} %copy-done), custom_call_target="tpu_custom_call" | custom-call | tf_op jit(solution)/shard_map/pallas_call | solution.py:413
  181.4 2.3 %copy.4 = f32[64,4,8,128]{3,2,1,0:T(8,128)} copy(f32[64,4,8,128]{3,2,1,0:T(8,128)} %bitcast.3) | data formatting | bytes 2097152
Async XLA Ops:
  28.5 1.2 copy-start.1
  29.7 1.0 copy-start.2
  152.6 1.0 copy-start

commit v2 on v1

--- a/solution.py
+++ b/solution.py
@@ -104,57 +104,6 @@
 
 W = (-205.0 / 72.0, 8.0 / 5.0, -1.0 / 5.0, 8.0 / 315.0, -1.0 / 560.0)
 
-def filter_kernel(v_ref, p_ref, o_ref, a_ref, b_ref):
-    step = 4
-    def fill(ref):
-        ref[:, 0:4] = ref[:, 128:132]
-        ref[:, 132:136] = ref[:, 4:8]
-    def level(src, prev, dst, gain):
-        scale = -0.5 * gain
-        w = [scale * c for c in W]
-        def body(t, carry):
-            base = t * step
-            pot = p_ref[pl.ds(base, step)]
-            diag = gain * (pot - 7.0) + 3.0 * w[0]
-            for o in range(2):
-                win = src[o, pl.ds(base, step + 8)]
-                v = win[4:4 + step]
-                acc = diag * v
-                u1 = pltpu.roll(v, 1, 1) + pltpu.roll(v, 7, 1)
-                r4 = pltpu.roll(v, 4, 1)
-                u2 = pltpu.roll(v + r4, 2, 1)
-                u3 = pltpu.roll(u1, 4, 1)
-                side = [u1, u2, u3, r4 + r4]
-                for m in range(1, 5):
-                    zz = pltpu.roll(v, m, 2) + pltpu.roll(v, 128 - m, 2)
-                    xx = win[4 + m:4 + m + step] + win[4 - m:4 - m + step]
-                    acc = acc + w[m] * (side[m - 1] + zz + xx)
-                if prev is not None:
-                    acc = acc - prev(o, base)
-                dst(o, base, acc)
-            return carry
-        lax.fori_loop(0, 128 // step, body, 0)
-    a_ref[:, 4:132] = v_ref[...]
-    fill(a_ref)
-    def into(ref, off):
-        def put(o, base, val):
-            ref[o, pl.ds(base + off, step)] = val
-        return put
-    def of(ref, off):
-        return lambda o, base: ref[o, pl.ds(base + off, step)]
-    level(a_ref, None, into(b_ref, 4), 0.25)
-    fill(b_ref)
-    level(b_ref, of(a_ref, 4), into(a_ref, 4), 0.5)
-    fill(a_ref)
-    level(a_ref, of(b_ref, 4), into(o_ref, 0), 0.5)
-
-def filt(v, p):
-    vm = pl.BlockSpec(memory_space=pltpu.VMEM)
-    return pl.pallas_call(filter_kernel, out_shape=jax.ShapeDtypeStruct(v.shape, jnp.float32),
-        in_specs=[vm, vm], out_specs=vm,
-        scratch_shapes=[pltpu.VMEM((2, 136, 8, 128), jnp.float32)] * 2,
-        compiler_params=pltpu.CompilerParams(vmem_limit_bytes=32 << 20))(v, p)
-
 MESH = pl.DeviceIdType.MESH
 
 
@@ -162,128 +111,172 @@
     return pl.BlockSpec(memory_space=pl.ANY)
 
 
-def spread_kernel(orb_ref, pot_ref, v_ref, p_ref, send, recv, psend, precv, own):
+STEP = 64
+
+
+def shift_matrix():
+    i = lax.broadcasted_iota(jnp.int32, (128, 128), 0)
+    j = lax.broadcasted_iota(jnp.int32, (128, 128), 1)
+    apart = jnp.abs(i - j)
+    apart = jnp.minimum(apart, 128 - apart)
+    out = jnp.zeros((128, 128), jnp.float32)
+    for m in range(1, 5):
+        out = jnp.where(apart == m, W[m], out)
+    return out
+
+
+def apply_level(src, pot_ref, along_z, gain, prev, put):
+    w = [-0.5 * gain * c for c in W]
+    shifts = along_z * (-0.5 * gain)
+
+    def body(t, carry):
+        base = t * STEP
+        win = src[pl.ds(base, STEP + 8)]
+        v = win[4:4 + STEP]
+        acc = (gain * (pot_ref[pl.ds(base, STEP)] - 7.0) + 3.0 * w[0]) * v
+        acc = acc + dot(v.reshape(STEP * 8, 128), shifts, NN).reshape(STEP, 8, 128)
+        u1 = pltpu.roll(v, 1, 1) + pltpu.roll(v, 7, 1)
+        r4 = pltpu.roll(v, 4, 1)
+        side = [u1, pltpu.roll(v + r4, 2, 1), pltpu.roll(u1, 4, 1), r4 + r4]
+        for m in range(1, 5):
+            xx = win[4 + m:4 + m + STEP] + win[4 - m:4 - m + STEP]
+            acc = acc + w[m] * (side[m - 1] + xx)
+        if prev is not None:
+            acc = acc - prev[pl.ds(base + 4, STEP)]
+        put(base, acc)
+        return carry
+
+    lax.fori_loop(0, 128 // STEP, body, 0)
+
+
+def fill(ref):
+    ref[0:4] = ref[128:132]
+    ref[132:136] = ref[4:8]
+
+
+def front_kernel(orb_ref, pot_ref, m_ref, a, b, pot, c, slab,
+                 send, recv, psend, precv, asend, arecv, bsend, brecv, own):
     me, my_orb = lax.axis_index("grid"), lax.axis_index("orb")
+    xy, z_lo = me // 2, lax.rem(me, 2)
+    z_hi, core = my_orb // 2, lax.rem(my_orb, 2)
+    zc = (z_hi * 2 + z_lo) * 2 + core
+
+    def stack(i):
+        z, k = i // 2, lax.rem(i, 2)
+        lo, hi = lax.rem(z, 2), z // 2
+        return (xy * 2 + lo, hi * 2 + k), lo, hi, k
+
     bar = pltpu.get_barrier_semaphore()
 
     def greet(d, carry):
         pl.semaphore_signal(bar, inc=1, device_id=(lax.rem(me + d, 32), my_orb), device_id_type=MESH)
         return carry
 
+    def greet_stack(d, carry):
+        pl.semaphore_signal(bar, inc=1, device_id=stack(lax.rem(zc + d, 16))[0], device_id_type=MESH)
+        return carry
+
     lax.fori_loop(1, 32, greet, 0)
-    pl.semaphore_wait(bar, 31)
-
-    def copies(d):
+    lax.fori_loop(1, 16, greet_stack, 0)
+    pl.semaphore_wait(bar, 46)
+
+    def orb_copy(k, d):
         to = lax.rem(me + d, 32)
-        field = pltpu.make_async_remote_copy(
-            src_ref=orb_ref.at[pl.ds(2 * to, 2)],
-            dst_ref=v_ref.at[:, pl.ds(4 * me, 4)],
-            send_sem=send.at[d], recv_sem=recv.at[d],
+        return pltpu.make_async_remote_copy(
+            src_ref=orb_ref.at[2 * to + k], dst_ref=a.at[k, pl.ds(4 + 4 * me, 4)],
+            send_sem=send.at[k, d], recv_sem=recv.at[k, d],
             device_id=(to, my_orb), device_id_type=MESH)
-        pot = pltpu.make_async_remote_copy(
-            src_ref=pot_ref, dst_ref=p_ref.at[pl.ds(4 * me, 4)],
+
+    def pot_copy(d):
+        return pltpu.make_async_remote_copy(
+            src_ref=pot_ref, dst_ref=pot.at[pl.ds(4 * me, 4)],
             send_sem=psend.at[d], recv_sem=precv.at[d],
-            device_id=(to, my_orb), device_id_type=MESH)
-        return field, pot
-
-    def start(d, carry):
-        for c in copies(d):
-            c.start()
-        return carry
-
-    lax.fori_loop(1, 32, start, 0)
-    mine = pltpu.make_async_copy(orb_ref.at[pl.ds(2 * me, 2)], v_ref.at[:, pl.ds(4 * me, 4)], own.at[0])
-    mine.start()
-    minep = pltpu.make_async_copy(pot_ref, p_ref.at[pl.ds(4 * me, 4)], own.at[1])
-    minep.start()
-    mine.wait()
-    minep.wait()
-
-    def finish(d, carry):
-        for c in copies(d):
-            c.wait()
-        return carry
-
-    lax.fori_loop(1, 32, finish, 0)
-
-
-def spread(orbitals, potential):
-    dma = pltpu.SemaphoreType.DMA
+            device_id=(lax.rem(me + d, 32), my_orb), device_id_type=MESH)
+
+    def plane_copy(k, d):
+        to = lax.rem(xy + d, 16)
+        return pltpu.make_async_remote_copy(
+            src_ref=c.at[k, pl.ds(8 * to, 8)], dst_ref=slab.at[k, xy],
+            send_sem=asend.at[k, d], recv_sem=arecv.at[k, d],
+            device_id=(to * 2 + z_lo, my_orb), device_id_type=MESH)
+
+    def cell_copy(k, d):
+        device, lo, hi, half = stack(lax.rem(zc + d, 16))
+        return pltpu.make_async_remote_copy(
+            src_ref=slab.at[k, :, 4 * lo + hi, half], dst_ref=m_ref.at[my_orb, :, z_lo, k],
+            send_sem=bsend.at[k, d], recv_sem=brecv.at[k, d],
+            device_id=device, device_id_type=MESH)
+
+    def each(first, last, do):
+        def body(d, carry):
+            do(d)
+            return carry
+        lax.fori_loop(first, last, body, 0)
+
+    def start_first(d):
+        orb_copy(0, d).start()
+        pot_copy(d).start()
+
+    each(1, 32, start_first)
+    each(1, 32, lambda d: orb_copy(1, d).start())
+    local = [pltpu.make_async_copy(orb_ref.at[2 * me + k], a.at[k, pl.ds(4 + 4 * me, 4)], own.at[k]) for k in range(2)]
+    local.append(pltpu.make_async_copy(pot_ref, pot.at[pl.ds(4 * me, 4)], own.at[2]))
+    for copy in local:
+        copy.start()
+    for copy in local:
+        copy.wait()
+
+    def wait_pot(d):
+        pot_copy(d).wait()
+
+    each(1, 32, wait_pot)
+    along_z = shift_matrix()
+    for k in range(2):
+        each(1, 32, lambda d: orb_copy(k, d).wait())
+        ak, bk, ck = a.at[k], b.at[k], c.at[k]
+
+        def put_b(base, value):
+            bk[pl.ds(base + 4, STEP)] = value
+
+        def put_a(base, value):
+            ak[pl.ds(base + 4, STEP)] = value
+
+        def put_c(base, value):
+            ck[pl.ds(base, STEP), 0] = value[:, 0:4]
+            ck[pl.ds(base, STEP), 1] = value[:, 4:8]
+
+        fill(ak)
+        apply_level(ak, pot, along_z, 0.25, None, put_b)
+        fill(bk)
+        apply_level(bk, pot, along_z, 0.5, ak, put_a)
+        fill(ak)
+        apply_level(ak, pot, along_z, 0.5, bk, put_c)
+        each(1, 16, lambda d: plane_copy(k, d).start())
+        mine = pltpu.make_async_copy(c.at[k, pl.ds(8 * xy, 8)], slab.at[k, xy], own.at[3 + k])
+        mine.start()
+        mine.wait()
+    for k in range(2):
+        each(1, 16, lambda d: plane_copy(k, d).wait())
+        each(1, 16, lambda d: cell_copy(k, d).start())
+        mine = pltpu.make_async_copy(slab.at[k, :, 4 * z_lo + z_hi, core], m_ref.at[my_orb, :, z_lo, k], own.at[5 + k])
+        mine.start()
+        mine.wait()
+    for k in range(2):
+        each(1, 16, lambda d: cell_copy(k, d).wait())
+
+
+def front(orbitals, potential):
+    dma, vmem, f32 = pltpu.SemaphoreType.DMA, pltpu.VMEM, jnp.float32
     return pl.pallas_call(
-        spread_kernel,
-        out_shape=(jax.ShapeDtypeStruct((2, 128, 8, 128), jnp.float32),
-                   jax.ShapeDtypeStruct((128, 8, 128), jnp.float32)),
-        in_specs=[any_spec()] * 2, out_specs=(any_spec(),) * 2,
-        scratch_shapes=[dma((32,))] * 4 + [dma((2,))],
-        compiler_params=pltpu.CompilerParams(collective_id=1, has_side_effects=True),
+        front_kernel,
+        out_shape=jax.ShapeDtypeStruct((8, 16, 2, 2, 4, 128), f32),
+        in_specs=[any_spec()] * 2, out_specs=any_spec(),
+        scratch_shapes=[vmem((2, 136, 8, 128), f32), vmem((2, 136, 8, 128), f32), vmem((128, 8, 128), f32),
+                        vmem((2, 128, 2, 4, 128), f32), vmem((2, 16, 8, 2, 4, 128), f32),
+                        dma((2, 32)), dma((2, 32)), dma((32,)), dma((32,)), dma((2, 16)), dma((2, 16)),
+                        dma((2, 16)), dma((2, 16)), dma((7,))],
+        compiler_params=pltpu.CompilerParams(collective_id=1, has_side_effects=True, vmem_limit_bytes=60 << 20),
     )(orbitals, potential)
-
-
-def collect_kernel(f_ref, m_ref, slab, send, recv, send2, recv2, own):
-    me, my_orb = lax.axis_index("grid"), lax.axis_index("orb")
-    bar = pltpu.get_barrier_semaphore()
-
-    def greet(d, carry):
-        pl.semaphore_signal(bar, inc=1, device_id=(lax.rem(me + d, 32), my_orb), device_id_type=MESH)
-        return carry
-
-    def greet_orb(d, carry):
-        pl.semaphore_signal(bar, inc=1, device_id=(me, lax.rem(my_orb + d, 8)), device_id_type=MESH)
-        return carry
-
-    lax.fori_loop(1, 32, greet, 0)
-    lax.fori_loop(1, 8, greet_orb, 0)
-    pl.semaphore_wait(bar, 38)
-
-    def piece(d):
-        to = lax.rem(me + d, 32)
-        return pltpu.make_async_remote_copy(
-            src_ref=f_ref.at[:, pl.ds(4 * to, 4)],
-            dst_ref=slab.at[pl.ds(2 * me, 2)],
-            send_sem=send.at[d], recv_sem=recv.at[d],
-            device_id=(to, my_orb), device_id_type=MESH)
-
-    def start(d, carry):
-        piece(d).start()
-        return carry
-
-    lax.fori_loop(1, 32, start, 0)
-    mine = pltpu.make_async_copy(f_ref.at[:, pl.ds(4 * me, 4)], slab.at[pl.ds(2 * me, 2)], own.at[0])
-    mine.start()
-    mine.wait()
-
-    def finish(d, carry):
-        piece(d).wait()
-        return carry
-
-    lax.fori_loop(1, 32, finish, 0)
-
-    def cells(d):
-        to = lax.rem(my_orb + d, 8)
-        return pltpu.make_async_remote_copy(
-            src_ref=slab.at[:, to // 2, lax.rem(to, 2)],
-            dst_ref=m_ref.at[pl.ds(64 * my_orb, 64)],
-            send_sem=send2.at[d], recv_sem=recv2.at[d],
-            device_id=(me, to), device_id_type=MESH)
-
-    for d in range(1, 8):
-        cells(d).start()
-    mine = pltpu.make_async_copy(slab.at[:, my_orb // 2, lax.rem(my_orb, 2)], m_ref.at[pl.ds(64 * my_orb, 64)], own.at[1])
-    mine.start()
-    mine.wait()
-    for d in range(1, 8):
-        cells(d).wait()
-
-
-def collect(f):
-    dma = pltpu.SemaphoreType.DMA
-    return pl.pallas_call(
-        collect_kernel,
-        out_shape=jax.ShapeDtypeStruct((512, 4, 128), jnp.float32),
-        in_specs=[any_spec()], out_specs=any_spec(),
-        scratch_shapes=[pltpu.VMEM((64, 4, 2, 4, 128), jnp.float32), dma((32,)), dma((32,)), dma((8,)), dma((8,)), dma((2,))],
-        compiler_params=pltpu.CompilerParams(collective_id=2, has_side_effects=True, vmem_limit_bytes=32 << 20),
-    )(f)
 
 
 def reduce_kernel(g_ref, out_ref, parts, zparts, send, recv, zsend, zrecv, asend, arecv, own):
@@ -420,9 +413,7 @@
 
 
 def per_device(orbitals, potential):
-    field, pot = spread(orbitals, potential)
-    filtered = filt(field, pot)
-    cells = collect(filtered.reshape(2, 128, 2, 4, 128))
+    cells = front(orbitals, potential).reshape(512, 4, 128)
     margin = reduce_all(margin_part(cells))
     rotated = rotate(margin, cells, 131072.0)
     return deliver(rotated).reshape(64, 4, 8, 128)

time: 185 us -> 160 us (0.86)
  Pallas kernels: 178 us -> 155 us
    pallas_call x3 -> x1, Pallas kernels: 90.8 us -> 65.3 us  [front(): pl.pallas_call(front_kernel, out_shape=jax.ShapeDtypeStruct((8, 16, 2, 2,...]
    pallas_call x1, Pallas kernels: 33.9 us -> 36 us  [reduce_all(): pl.pallas_call(reduce_kernel, out_shape=jax.ShapeDtypeStruct((1280, 128),...]
where the time goes in v2:
time: 160 us; the launch traced here: 159 us
  Pallas kernels  155 us (97%)
  local copies, waits for them, and re-layouts  4.45 us (3%)
    pallas_call x1, Pallas kernels, front(): pl.pallas_call(front_kernel, out_shape=jax.ShapeDtypeStruct((8, 16, 2, 2,...  65.3 us
    pallas_call x1, Pallas kernels, reduce_all(): pl.pallas_call(reduce_kernel, out_shape=jax.ShapeDtypeStruct((1280, 128),...  36 us
    pallas_call x1, Pallas kernels, deliver(): pl.pallas_call(deliver_kernel, out_shape=jax.ShapeDtypeStruct((64, 4, 2,...  28 us
    pallas_call x1, Pallas kernels, rotate(): pl.pallas_call(functools.partial(rotate_kernel, cells), out_shape=jax.Sha...  23.2 us
    unnamed x7, local copies, waits for them, and re-layouts  4.45 us

profile of v2, /device:TPU:1, one launch (start us, length us, event | category | flops | bytes accessed | tf_op | source)
XLA Modules:
  0.0 159.4 jit_solution(6807439870411537572)
XLA Ops:
  0.0 65.3 %shard_map.28 = f32[8,16,2,2,4,128]{5,4,3,2,1,0:T(4,128)} custom-call(f32[64,4,8,128]{3,2,1,0:T(8,128)} %orb_ref.1, f32[4,8,128]{2,1,0:T(8,128)} %pot_ref.1), custom_call_target="tpu_custom_call" | custom-call | tf_op jit(solution)/shard_map/pallas_call | solution.py:270
  65.3 0.0 copy-start
  65.3 1.2 copy-done
  66.6 2.4 %shard_map.29.g_ref = f32[1280,128]{1,0:T(8,128)S(1)} custom-call(f32[512,4,128]{2,1,0:T(4,128)S(1)} %bitcast.2), custom_call_target="tpu_custom_call" | custom-call | tf_op jit(solution)/shard_map/pallas_call | solution.py:101
  69.0 0.0 copy-start.1
  69.0 36.0 %shard_map.30.g_ref = f32[1280,128]{1,0:T(8,128)S(1)} custom-call(f32[1280,128]{1,0:T(8,128)S(1)} %shard_map.29.g_ref), custom_call_target="tpu_custom_call" | custom-call | tf_op jit(solution)/shard_map/pallas_call | solution.py:370
  105.0 0.0 copy-done.1
  105.0 23.2 %shard_map.31.y_ref = f32[512,4,128]{2,1,0:T(4,128)S(1)} custom-call(f32[1280,128]{1,0:T(8,128)S(1)} %shard_map.30.g_ref, f32[512,4,128]{2,1,0:T(4,128)S(1)} %bitcast.3), custom_call_target="tpu_custom_call" | custom-call | tf_op jit(solution)/shard_map/pallas_call | solution.py:85
  128.2 0.0 copy-start.2
  128.2 1.0 copy-done.2
  129.1 28.0 %shard_map.32 = f32[64,4,2,4,128]{4,3,2,1,0:T(4,128)} custom-call(f32[512,4,128]{2,1,0:T(4,128)} %copy-done.2), custom_call_target="tpu_custom_call" | custom-call | tf_op jit(solution)/shard_map/pallas_call | solution.py:406
  157.2 2.3 %copy.4 = f32[64,4,8,128]{3,2,1,0:T(8,128)} copy(f32[64,4,8,128]{3,2,1,0:T(8,128)} %bitcast.4) | data formatting | bytes 2097152
Async XLA Ops:
  65.3 1.2 copy-start
  69.0 36.0 %copy-start.1 = (f32[8,16,2,2,4,128]{5,4,3,2,1,0:T(4,128)S(1)}, f32[8,16,2,2,4,128]{5,4,3,2,1,0:T(4,128)}, u32[]{:S(2)}) copy-start(f32[8,16,2,2,4,128]{5,4,3,2,1,0:T(4,128)} %shard_map.28) | copy-start | bytes 3145732
  128.2 1.0 copy-start.2

commit v3 on v2

--- a/solution.py
+++ b/solution.py
@@ -19,7 +19,7 @@
     r = r * (2.0 - d * r)
     return r * (2.0 - d * r)
 
-def factor_block(s_ref, w_ref, base):
+def factor_block(s_ref, w_ref, base, half_done):
     sub = lax.broadcasted_iota(jnp.int32, (8, 128), 0)
     lane = lax.broadcasted_iota(jnp.int32, (8, 128), 1)
     s = [s_ref[pl.ds(base + 8 * i, 8), :] for i in range(16)]
@@ -43,7 +43,7 @@
             if j < 7:
                 sp = sp - m * s_rows[j]
                 wp = wp - m * w_rows[j]
-        w[p] = wp * lax.rsqrt(dvec)
+        w_ref[8 * p:8 * p + 8, :] = wp * lax.rsqrt(dvec)
         for i in range(p + 1, 16):
             raw = [jnp.broadcast_to(s[i][:, 8 * p + j:8 * p + j + 1], (8, 128)) for j in range(8)]
             si, wi = s[i], w[i]
@@ -54,53 +54,8 @@
                 si = si - m * s_rows[j]
                 wi = wi - m * w_rows[j]
             s[i], w[i] = si, wi
-    for i in range(16):
-        w_ref[8 * i:8 * i + 8, :] = w[i]
-
-def blk(i, j):
-    return i * (i + 1) // 2 + j
-
-def rotate_kernel(cells, g_ref, f_ref, y_ref, a_ref, x_ref, w_ref):
-    a_ref[...] = g_ref[...] * (1.0 / cells)
-    for q in range(4):
-        x_ref[:, 128 * q:128 * q + 128] = f_ref[:, q, :]
-    for b in range(4):
-        factor_block(a_ref, w_ref, 128 * blk(b, b))
-        w = w_ref[...]
-        low = {}
-        for i in range(b + 1, 4):
-            low[i] = dot(a_ref[pl.ds(128 * blk(i, b), 128), :], w, NT)
-            for j in range(b + 1, i + 1):
-                rows = pl.ds(128 * blk(i, j), 128)
-                a_ref[rows, :] = a_ref[rows, :] - dot(low[i], low[j], NT)
-        y = dot(w, x_ref[128 * b:128 * b + 128, :], NN)
-        for q in range(4):
-            y_ref[128 * b:128 * b + 128, q, :] = y[:, 128 * q:128 * q + 128]
-        for i in range(b + 1, 4):
-            rows = slice(128 * i, 128 * i + 128)
-            x_ref[rows, :] = x_ref[rows, :] - dot(low[i], y, NN)
-
-def rotate(g, f, cells):
-    vm = pl.BlockSpec(memory_space=pltpu.VMEM)
-    return pl.pallas_call(functools.partial(rotate_kernel, cells),
-        out_shape=jax.ShapeDtypeStruct((512, 4, 128), jnp.float32),
-        in_specs=[vm, vm], out_specs=vm,
-        scratch_shapes=[pltpu.VMEM((1280, 128), jnp.float32), pltpu.VMEM((512, 512), jnp.float32), pltpu.VMEM((128, 128), jnp.float32)],
-        compiler_params=pltpu.CompilerParams(vmem_limit_bytes=32 << 20))(g, f)
-
-def margin_kernel(f_ref, g_ref, x_ref):
-    for q in range(4):
-        x_ref[:, 128 * q:128 * q + 128] = f_ref[:, q, :]
-    for i in range(4):
-        xi = x_ref[128 * i:128 * i + 128, :]
-        for j in range(i + 1):
-            g_ref[pl.ds(128 * blk(i, j), 128), :] = dot(xi, x_ref[128 * j:128 * j + 128, :], NT)
-
-def margin_part(f):
-    vm = pl.BlockSpec(memory_space=pltpu.VMEM)
-    return pl.pallas_call(margin_kernel, out_shape=jax.ShapeDtypeStruct((1280, 128), jnp.float32),
-        in_specs=[vm], out_specs=vm, scratch_shapes=[pltpu.VMEM((512, 512), jnp.float32)],
-        compiler_params=pltpu.CompilerParams(vmem_limit_bytes=32 << 20))(f)
+        if p == 7:
+            half_done()
 
 W = (-205.0 / 72.0, 8.0 / 5.0, -1.0 / 5.0, 8.0 / 315.0, -1.0 / 560.0)
 
@@ -206,12 +161,6 @@
             src_ref=slab.at[k, :, 4 * lo + hi, half], dst_ref=m_ref.at[my_orb, :, z_lo, k],
             send_sem=bsend.at[k, d], recv_sem=brecv.at[k, d],
             device_id=device, device_id_type=MESH)
-
-    def each(first, last, do):
-        def body(d, carry):
-            do(d)
-            return carry
-        lax.fori_loop(first, last, body, 0)
 
     def start_first(d):
         orb_copy(0, d).start()
@@ -279,144 +228,201 @@
     )(orbitals, potential)
 
 
-def reduce_kernel(g_ref, out_ref, parts, zparts, send, recv, zsend, zrecv, asend, arecv, own):
+COLUMN = (0, 4, 7, 9)
+PIECES = ((0, 16), (512, 24))
+
+
+def blk(i, j):
+    return pl.ds(128 * (COLUMN[j] + i - j), 128)
+
+
+def each(first, last, do):
+    def body(d, carry):
+        do(d)
+        return carry
+    lax.fori_loop(first, last, body, 0)
+
+
+def back_kernel(cells, f_ref, out_ref, x_ref, g_ref, a_ref, y_ref, w_ref, cbuf, parts0, parts1, zparts0, zparts1,
+                csend, crecv, rsend, rrecv, zsend, zrecv, gsend, grecv, esend, erecv, dsend, drecv, own):
     me, my_orb = lax.axis_index("grid"), lax.axis_index("orb")
-    z_lo, z_hi = lax.rem(me, 2), my_orb // 2
-    at = (me // 2) * 2 + lax.rem(my_orb, 2)
-    zat = z_hi * 2 + z_lo
+    xy, z_lo = me // 2, lax.rem(me, 2)
+    z_hi, core = my_orb // 2, lax.rem(my_orb, 2)
+    z = z_hi * 2 + z_lo
+    parts, zparts = (parts0, parts1), (zparts0, zparts1)
+    partner = (me, z_hi * 2 + 1 - core)
 
     def plane(i):
-        return (i // 2) * 2 + z_lo, z_hi * 2 + lax.rem(i, 2)
-
-    def column(z):
-        return (me // 2) * 2 + lax.rem(z, 2), (z // 2) * 2 + lax.rem(my_orb, 2)
+        return (i * 2 + z_lo, my_orb)
+
+    def column(i):
+        return (xy * 2 + lax.rem(i, 2), (i // 2) * 2 + core)
 
     bar = pltpu.get_barrier_semaphore()
 
-    def greet(d, carry):
-        pl.semaphore_signal(bar, inc=1, device_id=plane(lax.rem(at + d, 32)), device_id_type=MESH)
-        return carry
-
-    def greet_z(d, carry):
-        pl.semaphore_signal(bar, inc=1, device_id=column(lax.rem(zat + d, 8)), device_id_type=MESH)
-        return carry
-
-    lax.fori_loop(1, 32, greet, 0)
-    lax.fori_loop(1, 8, greet_z, 0)
-    pl.semaphore_wait(bar, 38)
-
-    def scatter(d):
-        to = lax.rem(at + d, 32)
-        return pltpu.make_async_remote_copy(
-            src_ref=g_ref.at[pl.ds(pl.multiple_of(40 * to, 8), 40)], dst_ref=parts.at[at],
-            send_sem=send.at[d], recv_sem=recv.at[d],
-            device_id=plane(to), device_id_type=MESH)
-
-    def start(d, carry):
-        scatter(d).start()
-        return carry
-
-    lax.fori_loop(1, 32, start, 0)
-    my_rows = pl.ds(pl.multiple_of(40 * at, 8), 40)
-    parts[at] = g_ref[my_rows, :]
-
-    def finish(d, carry):
-        scatter(d).wait()
-        return carry
-
-    lax.fori_loop(1, 32, finish, 0)
-
-    def add(i, total):
-        return total + parts[i]
-
-    zparts[zat] = lax.fori_loop(1, 32, add, parts[0])
-
-    def exchange(d):
-        return pltpu.make_async_remote_copy(
-            src_ref=zparts.at[zat], dst_ref=zparts.at[zat],
-            send_sem=zsend.at[d], recv_sem=zrecv.at[d],
-            device_id=column(lax.rem(zat + d, 8)), device_id_type=MESH)
-
-    for d in range(1, 8):
-        exchange(d).start()
-    for d in range(1, 8):
-        exchange(d).wait()
-    total = zparts[0]
-    for z in range(1, 8):
-        total = total + zparts[z]
-    out_ref[my_rows, :] = total
-
-    def gather(d):
-        return pltpu.make_async_remote_copy(
-            src_ref=out_ref.at[my_rows], dst_ref=out_ref.at[my_rows],
-            send_sem=asend.at[d], recv_sem=arecv.at[d],
-            device_id=plane(lax.rem(at + d, 32)), device_id_type=MESH)
-
-    def start3(d, carry):
-        gather(d).start()
-        return carry
-
-    def finish3(d, carry):
-        gather(d).wait()
-        return carry
-
-    lax.fori_loop(1, 32, start3, 0)
-    lax.fori_loop(1, 32, finish3, 0)
-
-
-def reduce_all(g):
-    dma = pltpu.SemaphoreType.DMA
-    vm = pl.BlockSpec(memory_space=pltpu.VMEM)
+    def greet(device):
+        pl.semaphore_signal(bar, inc=1, device_id=device, device_id_type=MESH)
+
+    each(1, 16, lambda d: greet(plane(lax.rem(xy + d, 16))))
+    each(1, 8, lambda d: greet((me, lax.rem(my_orb + d, 8))))
+    each(0, 4, lambda d: greet((xy * 2 + 1 - z_lo, d * 2 + core)))
+
+    for q in range(4):
+        x_ref[:, 128 * q:128 * q + 128] = f_ref[:, q, :]
+
+    def gram(j):
+        xj = x_ref[128 * j:128 * j + 128, :]
+        for i in range(j, 4):
+            g_ref[blk(i, j), :] = dot(x_ref[128 * i:128 * i + 128, :], xj, NT)
+
+    def half_rows(p, which):
+        base, n = PIECES[p]
+        return pl.ds(pl.multiple_of(base + 16 * n * which, 8), 16 * n)
+
+    def own_rows(p, i):
+        base, n = PIECES[p]
+        return pl.ds(pl.multiple_of(base + 16 * n * core + n * i, 8), n)
+
+    def box(p):
+        return pl.ds(PIECES[p][0] // 2, 16 * PIECES[p][1])
+
+    def core_copy(p):
+        return pltpu.make_async_remote_copy(
+            src_ref=g_ref.at[half_rows(p, 1 - core)], dst_ref=cbuf.at[box(p)],
+            send_sem=csend.at[p], recv_sem=crecv.at[p], device_id=partner, device_id_type=MESH)
+
+    def scatter(p, d):
+        to = lax.rem(xy + d, 16)
+        return pltpu.make_async_remote_copy(
+            src_ref=g_ref.at[own_rows(p, to)], dst_ref=parts[p].at[xy],
+            send_sem=rsend.at[p, d], recv_sem=rrecv.at[p, d], device_id=plane(to), device_id_type=MESH)
+
+    def exchange(p, d):
+        return pltpu.make_async_remote_copy(
+            src_ref=zparts[p].at[z], dst_ref=zparts[p].at[z],
+            send_sem=zsend.at[p, d], recv_sem=zrecv.at[p, d],
+            device_id=column(lax.rem(z + d, 8)), device_id_type=MESH)
+
+    def gather(p, d):
+        return pltpu.make_async_remote_copy(
+            src_ref=a_ref.at[own_rows(p, xy)], dst_ref=a_ref.at[own_rows(p, xy)],
+            send_sem=gsend.at[p, d], recv_sem=grecv.at[p, d],
+            device_id=plane(lax.rem(xy + d, 16)), device_id_type=MESH)
+
+    def core_swap(p):
+        return pltpu.make_async_remote_copy(
+            src_ref=a_ref.at[half_rows(p, core)], dst_ref=a_ref.at[half_rows(p, core)],
+            send_sem=esend.at[p], recv_sem=erecv.at[p], device_id=partner, device_id_type=MESH)
+
+    def start_scatter(p):
+        core_copy(p).wait()
+        rows = half_rows(p, core)
+        g_ref[rows, :] = g_ref[rows, :] + cbuf[box(p), :]
+        each(1, 16, lambda d: scatter(p, d).start())
+        parts[p][xy] = g_ref[own_rows(p, xy), :]
+
+    def start_exchange(p):
+        each(1, 16, lambda d: scatter(p, d).wait())
+        total = parts[p][0]
+        for i in range(1, 16):
+            total = total + parts[p][i]
+        zparts[p][z] = total
+        each(1, 8, lambda d: exchange(p, d).start())
+
+    def start_gather(p):
+        each(1, 8, lambda d: exchange(p, d).wait())
+        total = zparts[p][0]
+        for i in range(1, 8):
+            total = total + zparts[p][i]
+        a_ref[own_rows(p, xy), :] = total * (1.0 / cells)
+        each(1, 16, lambda d: gather(p, d).start())
+
+    def start_swap(p):
+        each(1, 16, lambda d: gather(p, d).wait())
+        core_swap(p).start()
+
+    gram(0)
+    pl.semaphore_wait(bar, 26)
+    core_copy(0).start()
+    for j in range(1, 4):
+        gram(j)
+    core_copy(1).start()
+    for stage in (start_scatter, start_exchange, start_gather, start_swap):
+        for p in range(2):
+            stage(p)
+    core_swap(0).wait()
+
+    def rows_copy(to):
+        return pltpu.make_async_remote_copy(
+            src_ref=y_ref.at[pl.ds(64 * to, 64)], dst_ref=out_ref.at[:, z_hi, core],
+            send_sem=dsend.at[to], recv_sem=drecv.at[my_orb], device_id=(me, to), device_id_type=MESH)
+
+    def keep(to):
+        return pltpu.make_async_copy(y_ref.at[pl.ds(64 * to, 64)], out_ref.at[:, z_hi, core], own)
+
+    def rotate_rows(b, half):
+        to = 2 * b + half
+        y = dot(w_ref[64 * half:64 * half + 64, :], x_ref[128 * b:128 * b + 128, :], NN)
+        for q in range(4):
+            y_ref[64 * to:64 * to + 64, q, :] = y[:, 128 * q:128 * q + 128]
+
+        @pl.when(my_orb != to)
+        def _():
+            rows_copy(to).start()
+
+        @pl.when(my_orb == to)
+        def _():
+            keep(to).start()
+        return y
+
+    for b in range(4):
+        tops = []
+        factor_block(a_ref, w_ref, 128 * COLUMN[b], lambda: tops.append(rotate_rows(b, 0)))
+        w = w_ref[...]
+        if b == 0:
+            core_swap(1).wait()
+        low = {}
+        for i in range(b + 1, 4):
+            low[i] = dot(a_ref[blk(i, b), :], w, NT)
+            for j in range(b + 1, i + 1):
+                a_ref[blk(i, j), :] = a_ref[blk(i, j), :] - dot(low[i], low[j], NT)
+        y = jnp.concatenate([tops[0], rotate_rows(b, 1)], axis=0)
+        for i in range(b + 1, 4):
+            rows = slice(128 * i, 128 * i + 128)
+            x_ref[rows, :] = x_ref[rows, :] - dot(low[i], y, NN)
+
+    keep(0).wait()
+    for to in range(8):
+        @pl.when(my_orb != to)
+        def _():
+            rows_copy(to).wait_send()
+    for sender in range(8):
+        @pl.when(my_orb != sender)
+        def _():
+            pltpu.make_async_remote_copy(
+                src_ref=y_ref.at[pl.ds(0, 64)], dst_ref=out_ref.at[:, sender // 2, sender % 2],
+                send_sem=dsend.at[sender], recv_sem=drecv.at[sender],
+                device_id=(me, sender), device_id_type=MESH).wait_recv()
+
+
+def back(f, cells):
+    dma, vmem, f32 = pltpu.SemaphoreType.DMA, pltpu.VMEM, jnp.float32
     return pl.pallas_call(
-        reduce_kernel,
-        out_shape=jax.ShapeDtypeStruct((1280, 128), jnp.float32),
-        in_specs=[vm], out_specs=vm,
-        scratch_shapes=[pltpu.VMEM((32, 40, 128), jnp.float32), pltpu.VMEM((8, 40, 128), jnp.float32),
-                        dma((32,)), dma((32,)), dma((8,)), dma((8,)), dma((32,)), dma((32,)), dma((2,))],
-        compiler_params=pltpu.CompilerParams(collective_id=3, has_side_effects=True, vmem_limit_bytes=32 << 20),
-    )(g)
-
-
-def deliver_kernel(y_ref, out_ref, send, recv, own):
-    me, my_orb = lax.axis_index("grid"), lax.axis_index("orb")
-    bar = pltpu.get_barrier_semaphore()
-    for d in range(1, 8):
-        pl.semaphore_signal(bar, inc=1, device_id=(me, lax.rem(my_orb + d, 8)), device_id_type=MESH)
-    pl.semaphore_wait(bar, 7)
-
-    def rows(d):
-        to = lax.rem(my_orb + d, 8)
-        return pltpu.make_async_remote_copy(
-            src_ref=y_ref.at[pl.ds(64 * to, 64)],
-            dst_ref=out_ref.at[:, my_orb // 2, lax.rem(my_orb, 2)],
-            send_sem=send.at[d], recv_sem=recv.at[d],
-            device_id=(me, to), device_id_type=MESH)
-
-    for d in range(1, 8):
-        rows(d).start()
-    mine = pltpu.make_async_copy(y_ref.at[pl.ds(64 * my_orb, 64)], out_ref.at[:, my_orb // 2, lax.rem(my_orb, 2)], own.at[0])
-    mine.start()
-    mine.wait()
-    for d in range(1, 8):
-        rows(d).wait()
-
-
-def deliver(y):
-    dma = pltpu.SemaphoreType.DMA
-    return pl.pallas_call(
-        deliver_kernel,
-        out_shape=jax.ShapeDtypeStruct((64, 4, 2, 4, 128), jnp.float32),
-        in_specs=[any_spec()], out_specs=any_spec(),
-        scratch_shapes=[dma((8,)), dma((8,)), dma((1,))],
-        compiler_params=pltpu.CompilerParams(collective_id=4, has_side_effects=True),
-    )(y)
+        functools.partial(back_kernel, cells),
+        out_shape=jax.ShapeDtypeStruct((64, 4, 2, 4, 128), f32),
+        in_specs=[pl.BlockSpec(memory_space=pltpu.VMEM)], out_specs=any_spec(),
+        scratch_shapes=[vmem((512, 512), f32), vmem((1280, 128), f32), vmem((1280, 128), f32), vmem((512, 4, 128), f32),
+                        vmem((128, 128), f32), vmem((640, 128), f32), vmem((16, 16, 128), f32), vmem((16, 24, 128), f32),
+                        vmem((8, 16, 128), f32), vmem((8, 24, 128), f32),
+                        dma((2,)), dma((2,)), dma((2, 16)), dma((2, 16)), dma((2, 8)), dma((2, 8)),
+                        dma((2, 16)), dma((2, 16)), dma((2,)), dma((2,)), dma((8,)), dma((8,)), dma],
+        compiler_params=pltpu.CompilerParams(collective_id=2, has_side_effects=True, vmem_limit_bytes=32 << 20),
+    )(f)
 
 
 def per_device(orbitals, potential):
     cells = front(orbitals, potential).reshape(512, 4, 128)
-    margin = reduce_all(margin_part(cells))
-    rotated = rotate(margin, cells, 131072.0)
-    return deliver(rotated).reshape(64, 4, 8, 128)
+    return back(cells, 131072.0).reshape(64, 4, 8, 128)
 
 
 def solution(mesh):

time: 160 us -> 137 us (0.86)
  Pallas kernels: 155 us -> 134 us
  local copies, waits for them, and re-layouts: 4.45 us -> 2.19 us
    pallas_call x4 -> x1, Pallas kernels: 89.6 us -> 69.1 us  [back(): pl.pallas_call(functools.partial(back_kernel, cells), out_shape=jax.Shape...]
    unnamed x7 -> x3, local copies, waits for them, and re-layouts: 4.45 us -> 2.19 us
where the time goes in v3:
time: 137 us
  Pallas kernels  134 us (98%)
  local copies, waits for them, and re-layouts  2.19 us (2%)
    pallas_call x1, Pallas kernels, back(): pl.pallas_call(functools.partial(back_kernel, cells), out_shape=jax.Shape...  69.1 us
    pallas_call x1, Pallas kernels, front(): pl.pallas_call(front_kernel, out_shape=jax.ShapeDtypeStruct((8, 16, 2, 2,...  65.3 us

profile of v3, /device:TPU:1, one launch (start us, length us, event | category | flops | bytes accessed | tf_op | source)
XLA Modules:
  0.0 136.6 jit_solution(9492244782451437173)
XLA Ops:
  0.0 65.3 %shard_map.28 = f32[8,16,2,2,4,128]{5,4,3,2,1,0:T(4,128)} custom-call(f32[64,4,8,128]{3,2,1,0:T(8,128)} %orb_ref.1, f32[4,8,128]{2,1,0:T(8,128)} %pot_ref.1), custom_call_target="tpu_custom_call" | custom-call | tf_op jit(solution)/shard_map/pallas_call | solution.py:219
  65.3 0.0 copy-start
  65.3 1.2 copy-done
  66.6 69.1 %shard_map.29 = f32[64,4,2,4,128]{4,3,2,1,0:T(4,128)S(1)} custom-call(f32[512,4,128]{2,1,0:T(4,128)S(1)} %bitcast.3), custom_call_target="tpu_custom_call" | custom-call | tf_op jit(solution)/shard_map/pallas_call | solution.py:410
  135.7 1.0 copy.4
Async XLA Ops:
  65.3 1.2 copy-start

commit v4 on v3

v4 whole, which is shorter than its diff:
```python
import functools
import jax, jax.numpy as jnp
from jax import lax
from jax.sharding import PartitionSpec as P
from jax.experimental import pallas as pl
from jax.experimental.pallas import tpu as pltpu
HI = lax.Precision.HIGHEST
NT = (((1,), (1,)), ((), ()))
NN = (((1,), (0,)), ((), ()))

def dot(a, b, dims):
    return lax.dot_general(a, b, dims, precision=HI, preferred_element_type=jnp.float32)

def row_of(block, j):
    return jnp.broadcast_to(block[j:j + 1, :], (8, 128))

def recip(d):
    r = pl.reciprocal(d, approx=True)
    return r * (2.0 - d * r)

def factor_block(s_ref, w_ref, base, half_done):
    sub = lax.broadcasted_iota(jnp.int32, (8, 128), 0)
    lane = lax.broadcasted_iota(jnp.int32, (8, 128), 1)
    s = [s_ref[pl.ds(base + 8 * i, 8), :] for i in range(16)]
    w = [jnp.where(lane == sub + 8 * i, 1.0, 0.0).astype(jnp.float32) for i in range(16)]
    for p in range(16):
        col = [jnp.broadcast_to(s[p][:, 8 * p + j:8 * p + j + 1], (8, 128)) for j in range(8)]
        fac, rinv, s_rows, w_rows = {}, [], [], []
        sp, wp = s[p], w[p]
        dvec = jnp.ones((8, 128), jnp.float32)
        for j in range(8):
            d = row_of(col[j], j)
            below = jnp.where(sub > j, col[j], 0.0)
            r = recip(d)
            rinv.append(r)
            dvec = jnp.where(sub == j, d, dvec)
            m = below * r
            for k in range(j + 1, 8):
                fac[j, k] = row_of(col[k], j)
                col[k] = col[k] - m * fac[j, k]
            s_rows.append(row_of(sp, j))
            w_rows.append(row_of(wp, j))
            if j < 7:
                sp = sp - m * s_rows[j]
                wp = wp - m * w_rows[j]
        w_ref[8 * p:8 * p + 8, :] = wp * lax.rsqrt(dvec)
        for i in range(p + 1, 16):
            raw = [jnp.broadcast_to(s[i][:, 8 * p + j:8 * p + j + 1], (8, 128)) for j in range(8)]
            si, wi = s[i], w[i]
            for j in range(8):
                m = raw[j] * rinv[j]
                for k in range(j + 1, 8):
                    raw[k] = raw[k] - m * fac[j, k]
                si = si - m * s_rows[j]
                wi = wi - m * w_rows[j]
            s[i], w[i] = si, wi
        if p == 7:
            half_done()

W = (-205.0 / 72.0, 8.0 / 5.0, -1.0 / 5.0, 8.0 / 315.0, -1.0 / 560.0)

MESH = pl.DeviceIdType.MESH


def any_spec():
    return pl.BlockSpec(memory_space=pl.ANY)


STEP = 64


def shift_matrix():
    i = lax.broadcasted_iota(jnp.int32, (128, 128), 0)
    j = lax.broadcasted_iota(jnp.int32, (128, 128), 1)
    apart = jnp.abs(i - j)
    apart = jnp.minimum(apart, 128 - apart)
    out = jnp.zeros((128, 128), jnp.float32)
    for m in range(1, 5):
        out = jnp.where(apart == m, W[m], out)
    return out


def apply_level(src, pot_ref, along_z, gain, prev, put):
    w = [-0.5 * gain * c for c in W]
    shifts = along_z * (-0.5 * gain)

    def body(t, carry):
        base = t * STEP
        win = src[pl.ds(base, STEP + 8)]
        v = win[4:4 + STEP]
        acc = (gain * (pot_ref[pl.ds(base, STEP)] - 7.0) + 3.0 * w[0]) * v
        acc = acc + dot(v.reshape(STEP * 8, 128), shifts, NN).reshape(STEP, 8, 128)
        u1 = pltpu.roll(v, 1, 1) + pltpu.roll(v, 7, 1)
        r4 = pltpu.roll(v, 4, 1)
        side = [u1, pltpu.roll(v + r4, 2, 1), pltpu.roll(u1, 4, 1), r4 + r4]
        for m in range(1, 5):
            xx = win[4 + m:4 + m + STEP] + win[4 - m:4 - m + STEP]
            acc = acc + w[m] * (side[m - 1] + xx)
        if prev is not None:
            acc = acc - prev[pl.ds(base + 4, STEP)]
        put(base, acc)
        return carry

    lax.fori_loop(0, 128 // STEP, body, 0)


def fill(ref):
    ref[0:4] = ref[128:132]
    ref[132:136] = ref[4:8]


COLUMN = (0, 4, 7, 9)
PIECES = ((0, 16), (512, 24))
CELLS = 128.0 * 8.0 * 128.0


def blk(i, j):
    return pl.ds(128 * (COLUMN[j] + i - j), 128)


def each(first, last, do):
    def body(d, carry):
        do(d)
        return carry
    lax.fori_loop(first, last, body, 0)


def wait_bytes(like, sem):
    pltpu.make_async_copy(like, like, sem).wait()


def mega_kernel(orb_ref, pot_ref, out_ref, a, b, pot5, c, slab, m6, x_ref, g_ref, a_ref, y_ref, w_ref, cbuf,
                parts0, parts1, zparts0, zparts1, send, recv, psend, precv, asend, arecv, bsend, brecv, own,
                csend, crecv, rsend, rrecv, zsend, zrecv, gsend, grecv, esend, erecv, dsend, drecv):
    me, my_orb = lax.axis_index("grid"), lax.axis_index("orb")
    xy, z_lo = me // 2, lax.rem(me, 2)
    z_hi, core = my_orb // 2, lax.rem(my_orb, 2)
    z = z_hi * 2 + z_lo
    zc = z * 2 + core
    pot = pot5.reshape(128, 8, 128)
    parts, zparts = (parts0, parts1), (zparts0, zparts1)
    partner = (me, z_hi * 2 + 1 - core)

    def stack(i):
        at, k = i // 2, lax.rem(i, 2)
        lo, hi = lax.rem(at, 2), at // 2
        return (xy * 2 + lo, hi * 2 + k), lo, hi, k

    def plane(i):
        return (i * 2 + z_lo, my_orb)

    def column(i):
        return (xy * 2 + lax.rem(i, 2), (i // 2) * 2 + core)

    bar = pltpu.get_barrier_semaphore()

    def greet(device):
        pl.semaphore_signal(bar, inc=1, device_id=device, device_id_type=MESH)

    each(1, 32, lambda d: greet((lax.rem(me + d, 32), my_orb)))
    each(1, 16, lambda d: greet(stack(lax.rem(zc + d, 16))[0]))

    def remote(src, dst, send_sem, recv_sem, device):
        return pltpu.make_async_remote_copy(src_ref=src, dst_ref=dst, send_sem=send_sem, recv_sem=recv_sem,
                                            device_id=device, device_id_type=MESH)

    def pot_copy(d):
        half = pl.ds(2 * core, 2)
        remote(pot_ref.at[half], pot5.at[me, core], psend, precv, (lax.rem(me + 9 * d, 32), my_orb)).start()

    def orb_copy(k, d):
        to = lax.rem(me + 9 * d, 32)
        remote(orb_ref.at[2 * to + k], a.at[k, pl.ds(4 + 4 * me, 4)], send.at[k], recv.at[k], (to, my_orb)).start()

    pot_own = pltpu.make_async_copy(pot_ref.at[pl.ds(2 * core, 2)], pot5.at[me, core], own.at[2])
    pot_own.start()
    local = [pltpu.make_async_copy(orb_ref.at[2 * me + k], a.at[k, pl.ds(4 + 4 * me, 4)], own.at[k]) for k in range(2)]
    for copy in local:
        copy.start()
    pl.semaphore_wait(bar, 46)
    each(1, 32, pot_copy)
    each(1, 32, lambda d: orb_copy(0, d))
    each(1, 32, lambda d: orb_copy(1, d))
    pot_own.wait()
    wait_bytes(pot5.at[pl.ds(0, 31), 0], precv)
    pot_swap = remote(pot5.at[:, core], pot5.at[:, core], esend.at[2], erecv.at[2], partner)
    pot_swap.start()
    for copy in local:
        copy.wait()
    along_z = shift_matrix()

    def plane_copy(k, d):
        to = lax.rem(xy + 5 * d, 16)
        remote(c.at[k, pl.ds(8 * to, 8)], slab.at[k, xy], asend.at[k], arecv.at[k], plane(to)).start()

    def cell_copy(k, d):
        device, lo, hi, half = stack(lax.rem(zc + 7 * d, 16))
        remote(slab.at[k, :, 4 * lo + hi, half], m6.at[my_orb, :, z_lo, k], bsend.at[k], brecv.at[k], device).start()

    for k in range(2):
        wait_bytes(a.at[k, pl.ds(0, 124)], recv.at[k])
        if k == 0:
            pot_swap.wait()
        ak, bk, ck = a.at[k], b.at[k], c.at[k]

        def put_b(base, value):
            bk[pl.ds(base + 4, STEP)] = value

        def put_a(base, value):
            ak[pl.ds(base + 4, STEP)] = value

        def put_c(base, value):
            ck[pl.ds(base, STEP), 0] = value[:, 0:4]
            ck[pl.ds(base, STEP), 1] = value[:, 4:8]

        fill(ak)
        apply_level(ak, pot, along_z, 0.25, None, put_b)
        fill(bk)
        apply_level(bk, pot, along_z, 0.5, ak, put_a)
        fill(ak)
        apply_level(ak, pot, along_z, 0.5, bk, put_c)
        each(1, 16, lambda d: plane_copy(k, d))
        mine = pltpu.make_async_copy(c.at[k, pl.ds(8 * xy, 8)], slab.at[k, xy], own.at[3 + k])
        mine.start()
        mine.wait()
    for k in range(2):
        wait_bytes(slab.at[k, pl.ds(0, 15)], arecv.at[k])
        each(1, 16, lambda d: cell_copy(k, d))
        mine = pltpu.make_async_copy(slab.at[k, :, 4 * z_lo + z_hi, core], m6.at[my_orb, :, z_lo, k], own.at[5 + k])
        mine.start()
        mine.wait()
    for k in range(2):
        wait_bytes(slab.at[k, pl.ds(0, 15)], brecv.at[k])

    f_ref = m6.reshape(512, 4, 128)
    for q in range(4):
        x_ref[:, 128 * q:128 * q + 128] = f_ref[:, q, :]

    def gram(j):
        xj = x_ref[128 * j:128 * j + 128, :]
        for i in range(j, 4):
            g_ref[blk(i, j), :] = dot(x_ref[128 * i:128 * i + 128, :], xj, NT)

    def half_rows(p, which):
        base, n = PIECES[p]
        return pl.ds(pl.multiple_of(base + 16 * n * which, 8), 16 * n)

    def own_rows(p, i):
        base, n = PIECES[p]
        return pl.ds(pl.multiple_of(base + 16 * n * core + n * i, 8), n)

    def box(p):
        return pl.ds(PIECES[p][0] // 2, 16 * PIECES[p][1])

    def core_copy(p):
        return remote(g_ref.at[half_rows(p, 1 - core)], cbuf.at[box(p)], csend.at[p], crecv.at[p], partner)

    def scatter(p, d):
        to = lax.rem(xy + 5 * d, 16)
        remote(g_ref.at[own_rows(p, to)], parts[p].at[xy], rsend.at[p], rrecv.at[p], plane(to)).start()

    def exchange(p, d):
        remote(zparts[p].at[z], zparts[p].at[z], zsend.at[p], zrecv.at[p], column(lax.rem(z + 3 * d, 8))).start()

    def gather(p, d):
        rows = a_ref.at[own_rows(p, xy)]
        remote(rows, rows, gsend.at[p], grecv.at[p], plane(lax.rem(xy + 5 * d, 16))).start()

    def core_swap(p):
        rows = a_ref.at[half_rows(p, core)]
        return remote(rows, rows, esend.at[p], erecv.at[p], partner)

    def start_scatter(p):
        core_copy(p).wait()
        rows = half_rows(p, core)
        g_ref[rows, :] = g_ref[rows, :] + cbuf[box(p), :]
        each(1, 16, lambda d: scatter(p, d))
        parts[p][xy] = g_ref[own_rows(p, xy), :]

    def start_exchange(p):
        wait_bytes(parts[p].at[pl.ds(0, 15)], rrecv.at[p])
        total = parts[p][0]
        for i in range(1, 16):
            total = total + parts[p][i]
        zparts[p][z] = total
        each(1, 8, lambda d: exchange(p, d))

    def start_gather(p):
        wait_bytes(zparts[p].at[pl.ds(0, 7)], zrecv.at[p])
        total = zparts[p][0]
        for i in range(1, 8):
            total = total + zparts[p][i]
        a_ref[own_rows(p, xy), :] = total * (1.0 / CELLS)
        each(1, 16, lambda d: gather(p, d))

    def start_swap(p):
        wait_bytes(parts[p].at[pl.ds(0, 15)], grecv.at[p])
        wait_bytes(parts[p].at[pl.ds(0, 15)], gsend.at[p])
        core_swap(p).start()

    gram(0)
    core_copy(0).start()
    for j in range(1, 4):
        gram(j)
    core_copy(1).start()
    for stage in (start_scatter, start_exchange, start_gather, start_swap):
        for p in range(2):
            stage(p)
    core_swap(0).wait()

    def rows_copy(to):
        return remote(y_ref.at[pl.ds(64 * to, 64)], out_ref.at[:, z_hi, core], dsend, drecv, (me, to))

    def keep(to):
        return pltpu.make_async_copy(y_ref.at[pl.ds(64 * to, 64)], out_ref.at[:, z_hi, core], own.at[7])

    def rotate_rows(b, half):
        to = 2 * b + half
        y = dot(w_ref[64 * half:64 * half + 64, :], x_ref[128 * b:128 * b + 128, :], NN)
        for q in range(4):
            y_ref[64 * to:64 * to + 64, q, :] = y[:, 128 * q:128 * q + 128]

        @pl.when(my_orb != to)
        def _():
            rows_copy(to).start()

        @pl.when(my_orb == to)
        def _():
            keep(to).start()
        return y

    for b in range(4):
        tops = []
        factor_block(a_ref, w_ref, 128 * COLUMN[b], lambda: tops.append(rotate_rows(b, 0)))
        w = w_ref[...]
        if b == 0:
            core_swap(1).wait()
        low = {}
        for i in range(b + 1, 4):
            low[i] = dot(a_ref[blk(i, b), :], w, NT)
            for j in range(b + 1, i + 1):
                a_ref[blk(i, j), :] = a_ref[blk(i, j), :] - dot(low[i], low[j], NT)
        y = jnp.concatenate([tops[0], rotate_rows(b, 1)], axis=0)
        for i in range(b + 1, 4):
            rows = slice(128 * i, 128 * i + 128)
            x_ref[rows, :] = x_ref[rows, :] - dot(low[i], y, NN)

    wait_bytes(pot5.at[pl.ds(0, 31), 0], psend)
    for k in range(2):
        wait_bytes(a.at[k, pl.ds(0, 124)], send.at[k])
        wait_bytes(slab.at[k, pl.ds(0, 15)], asend.at[k])
        wait_bytes(slab.at[k, pl.ds(0, 15)], bsend.at[k])
    for p in range(2):
        wait_bytes(parts[p].at[pl.ds(0, 15)], rsend.at[p])
        wait_bytes(zparts[p].at[pl.ds(0, 7)], zsend.at[p])
    keep(0).wait()
    wait_bytes(y_ref.at[pl.ds(0, 448)], dsend)
    wait_bytes(y_ref.at[pl.ds(0, 448)], drecv)


def mega(orbitals, potential):
    dma, f32 = pltpu.SemaphoreType.DMA, jnp.float32

    def vmem(*shape):
        return pltpu.VMEM(shape, f32)

    return pl.pallas_call(
        mega_kernel,
        out_shape=jax.ShapeDtypeStruct((64, 4, 2, 4, 128), f32),
        in_specs=[any_spec()] * 2, out_specs=any_spec(),
        scratch_shapes=[vmem(2, 136, 8, 128), vmem(2, 136, 8, 128), vmem(32, 2, 2, 8, 128), vmem(2, 128, 2, 4, 128),
                        vmem(2, 16, 8, 2, 4, 128), vmem(8, 16, 2, 2, 4, 128),
                        vmem(512, 512), vmem(1280, 128), vmem(1280, 128), vmem(512, 4, 128), vmem(128, 128),
                        vmem(640, 128), vmem(16, 16, 128), vmem(16, 24, 128), vmem(8, 16, 128), vmem(8, 24, 128),
                        dma((2,)), dma((2,)), dma, dma, dma((2,)), dma((2,)), dma((2,)), dma((2,)), dma((8,)),
                        dma((2,)), dma((2,)), dma((2,)), dma((2,)), dma((2,)), dma((2,)),
                        dma((2,)), dma((2,)), dma((3,)), dma((3,)), dma, dma],
        compiler_params=pltpu.CompilerParams(collective_id=1, has_side_effects=True, vmem_limit_bytes=32 << 20),
    )(orbitals, potential)


def per_device(orbitals, potential):
    return mega(orbitals, potential).reshape(64, 4, 8, 128)


def solution(mesh):
    in_specs = (P("orb", "grid", None, None), P("grid", None, None))
    out_specs = P("orb", "grid", None, None)
    return jax.shard_map(
        per_device, mesh=mesh, in_specs=in_specs, out_specs=out_specs, check_vma=False
    )
```

time: 137 us -> 124 us (0.905)
  Pallas kernels: 134 us -> 120 us
    pallas_call x2 -> x1, Pallas kernels: 134 us -> 120 us  [mega(): pl.pallas_call(mega_kernel, out_shape=jax.ShapeDtypeStruct((64, 4, 2, 4,...]
    unnamed x3 -> x5, local copies, waits for them, and re-layouts: 2.19 us -> 2.91 us
where the time goes in v4:
time: 124 us; the launch traced here: 123 us
  Pallas kernels  120 us (97%)
  local copies, waits for them, and re-layouts  2.91 us (2%)
    pallas_call x1, Pallas kernels, mega(): pl.pallas_call(mega_kernel, out_shape=jax.ShapeDtypeStruct((64, 4, 2, 4,...  120 us
    unnamed x5, local copies, waits for them, and re-layouts  2.91 us

profile of v4, /device:TPU:1, one launch (start us, length us, event | category | flops | bytes accessed | tf_op | source)
XLA Modules:
  0.0 123.1 jit_solution(17873515799170308082)
XLA Ops:
  0.0 0.0 copy-start
  0.0 1.2 copy-done
  1.2 0.0 copy-start.1
  1.2 0.7 copy-done.1
  1.9 120.2 %shard_map.28 = f32[64,4,2,4,128]{4,3,2,1,0:T(4,128)S(1)} custom-call(f32[64,4,8,128]{3,2,1,0:T(8,128)S(1)} %copy-done, f32[4,8,128]{2,1,0:T(8,128)S(1)} %copy-done.1), custom_call_target="tpu_custom_call" | custom-call | tf_op jit(solution)/shard_map/pallas_call | solution.py:367
  122.1 1.0 copy.4
Async XLA Ops:
  0.0 1.2 copy-start
  1.2 0.7 copy-start.1

commit v5 on v4

--- a/solution.py
+++ b/solution.py
@@ -18,7 +18,7 @@
     r = pl.reciprocal(d, approx=True)
     return r * (2.0 - d * r)
 
-def factor_block(s_ref, w_ref, base, half_done):
+def factor_block(s_ref, w_ref, base, after):
     sub = lax.broadcasted_iota(jnp.int32, (8, 128), 0)
     lane = lax.broadcasted_iota(jnp.int32, (8, 128), 1)
     s = [s_ref[pl.ds(base + 8 * i, 8), :] for i in range(16)]
@@ -28,10 +28,13 @@
         fac, rinv, s_rows, w_rows = {}, [], [], []
         sp, wp = s[p], w[p]
         dvec = jnp.ones((8, 128), jnp.float32)
-        for j in range(8):
-            d = row_of(col[j], j)
-            below = jnp.where(sub > j, col[j], 0.0)
-            r = recip(d)
+        first = col[0]
+        for j in range(1, 8):
+            first = jnp.where(sub == j, col[j], first)
+        scale = pl.reciprocal(first, approx=True)
+
+        def eliminate(j, d, r, below):
+            nonlocal sp, wp, dvec
             rinv.append(r)
             dvec = jnp.where(sub == j, d, dvec)
             m = below * r
@@ -43,6 +46,15 @@
             if j < 7:
                 sp = sp - m * s_rows[j]
                 wp = wp - m * w_rows[j]
+
+        for j in range(0, 8, 2):
+            d0, off, d1 = row_of(col[j], j), row_of(col[j + 1], j), row_of(col[j + 1], j + 1)
+            k0 = row_of(scale, j)
+            d0k = d0 * k0
+            both = d0k * d1 - (off * k0) * off
+            r0, rb = recip(d0), recip(both)
+            eliminate(j, d0, r0, jnp.where(sub > j, col[j], 0.0))
+            eliminate(j + 1, both / d0k, d0k * rb, jnp.where(sub > j + 1, col[j + 1], 0.0))
         w_ref[8 * p:8 * p + 8, :] = wp * lax.rsqrt(dvec)
         for i in range(p + 1, 16):
             raw = [jnp.broadcast_to(s[i][:, 8 * p + j:8 * p + j + 1], (8, 128)) for j in range(8)]
@@ -54,8 +66,8 @@
                 si = si - m * s_rows[j]
                 wi = wi - m * w_rows[j]
             s[i], w[i] = si, wi
-        if p == 7:
-            half_done()
+        if p in after:
+            after[p]()
 
 W = (-205.0 / 72.0, 8.0 / 5.0, -1.0 / 5.0, 8.0 / 315.0, -1.0 / 560.0)
 
@@ -189,13 +201,18 @@
         copy.wait()
     along_z = shift_matrix()
 
-    def plane_copy(k, d):
+    lows = (1 - z_lo, z_lo)
+
+    def plane_copy(k, s, d):
         to = lax.rem(xy + 5 * d, 16)
-        remote(c.at[k, pl.ds(8 * to, 8)], slab.at[k, xy], asend.at[k], arecv.at[k], plane(to)).start()
-
-    def cell_copy(k, d):
-        device, lo, hi, half = stack(lax.rem(zc + 7 * d, 16))
-        remote(slab.at[k, :, 4 * lo + hi, half], m6.at[my_orb, :, z_lo, k], bsend.at[k], brecv.at[k], device).start()
+        planes = pl.ds(4 * lows[s], 4)
+        remote(c.at[k, pl.ds(8 * to + 4 * lows[s], 4)], slab.at[k, xy, planes],
+               asend.at[k, s], arecv.at[k, s], plane(to)).start()
+
+    def cell_copy(k, s, d):
+        to = lax.rem(my_orb + 3 * d, 8)
+        remote(slab.at[k, :, 4 * lows[s] + to // 2, lax.rem(to, 2)], m6.at[my_orb, :, z_lo, k],
+               bsend.at[k], brecv.at[k], (xy * 2 + lows[s], to)).start()
 
     for k in range(2):
         wait_bytes(a.at[k, pl.ds(0, 124)], recv.at[k])
@@ -219,13 +236,15 @@
         apply_level(bk, pot, along_z, 0.5, ak, put_a)
         fill(ak)
         apply_level(ak, pot, along_z, 0.5, bk, put_c)
-        each(1, 16, lambda d: plane_copy(k, d))
+        for s in range(2):
+            each(1, 16, lambda d: plane_copy(k, s, d))
         mine = pltpu.make_async_copy(c.at[k, pl.ds(8 * xy, 8)], slab.at[k, xy], own.at[3 + k])
         mine.start()
         mine.wait()
     for k in range(2):
-        wait_bytes(slab.at[k, pl.ds(0, 15)], arecv.at[k])
-        each(1, 16, lambda d: cell_copy(k, d))
+        for s in range(2):
+            wait_bytes(slab.at[k, pl.ds(0, 15), pl.ds(0, 4)], arecv.at[k, s])
+            each(s, 8, lambda d: cell_copy(k, s, d))
         mine = pltpu.make_async_copy(slab.at[k, :, 4 * z_lo + z_hi, core], m6.at[my_orb, :, z_lo, k], own.at[5 + k])
         mine.start()
         mine.wait()
@@ -329,26 +348,48 @@
             keep(to).start()
         return y
 
+    soon, later = [], []
     for b in range(4):
         tops = []
-        factor_block(a_ref, w_ref, 128 * COLUMN[b], lambda: tops.append(rotate_rows(b, 0)))
+
+        def run(work):
+            while work:
+                work.pop(0)()
+
+        factor_block(a_ref, w_ref, 128 * COLUMN[b], {
+            0: lambda: run(soon), 7: lambda: tops.append(rotate_rows(b, 0)), 8: lambda: run(later)})
         w = w_ref[...]
         if b == 0:
             core_swap(1).wait()
         low = {}
-        for i in range(b + 1, 4):
+
+        def lower(i, b=b, w=w, low=low):
             low[i] = dot(a_ref[blk(i, b), :], w, NT)
-            for j in range(b + 1, i + 1):
-                a_ref[blk(i, j), :] = a_ref[blk(i, j), :] - dot(low[i], low[j], NT)
+
+        def update(i, j, low=low):
+            a_ref[blk(i, j), :] = a_ref[blk(i, j), :] - dot(low[i], low[j], NT)
+
+        if b < 3:
+            lower(b + 1)
+            update(b + 1, b + 1)
         y = jnp.concatenate([tops[0], rotate_rows(b, 1)], axis=0)
-        for i in range(b + 1, 4):
+
+        def solve(i, y=y, low=low):
             rows = slice(128 * i, 128 * i + 128)
             x_ref[rows, :] = x_ref[rows, :] - dot(low[i], y, NN)
+
+        for i in range(b + 1, 4):
+            if i > b + 1:
+                later.append(functools.partial(lower, i))
+                for j in range(b + 1, i + 1):
+                    later.append(functools.partial(update, i, j))
+            (later if i > b + 1 else soon).append(functools.partial(solve, i))
 
     wait_bytes(pot5.at[pl.ds(0, 31), 0], psend)
     for k in range(2):
         wait_bytes(a.at[k, pl.ds(0, 124)], send.at[k])
-        wait_bytes(slab.at[k, pl.ds(0, 15)], asend.at[k])
+        for s in range(2):
+            wait_bytes(slab.at[k, pl.ds(0, 15), pl.ds(0, 4)], asend.at[k, s])
         wait_bytes(slab.at[k, pl.ds(0, 15)], bsend.at[k])
     for p in range(2):
         wait_bytes(parts[p].at[pl.ds(0, 15)], rsend.at[p])
@@ -372,7 +413,7 @@
                         vmem(2, 16, 8, 2, 4, 128), vmem(8, 16, 2, 2, 4, 128),
                         vmem(512, 512), vmem(1280, 128), vmem(1280, 128), vmem(512, 4, 128), vmem(128, 128),
                         vmem(640, 128), vmem(16, 16, 128), vmem(16, 24, 128), vmem(8, 16, 128), vmem(8, 24, 128),
-                        dma((2,)), dma((2,)), dma, dma, dma((2,)), dma((2,)), dma((2,)), dma((2,)), dma((8,)),
+                        dma((2,)), dma((2,)), dma, dma, dma((2, 2)), dma((2, 2)), dma((2,)), dma((2,)), dma((8,)),
                         dma((2,)), dma((2,)), dma((2,)), dma((2,)), dma((2,)), dma((2,)),
                         dma((2,)), dma((2,)), dma((3,)), dma((3,)), dma, dma],
         compiler_params=pltpu.CompilerParams(collective_id=1, has_side_effects=True, vmem_limit_bytes=32 << 20),

time: 124 us -> 119 us (0.960)
  Pallas kernels: 120 us -> 115 us
    pallas_call x1, Pallas kernels: 120 us -> 115 us  [mega(): pl.pallas_call(mega_kernel, out_shape=jax.ShapeDtypeStruct((64, 4, 2, 4,...]
where the time goes in v5:
time: 119 us; the launch traced here: 118 us
  Pallas kernels  115 us (97%)
  local copies, waits for them, and re-layouts  2.91 us (2%)
    pallas_call x1, Pallas kernels, mega(): pl.pallas_call(mega_kernel, out_shape=jax.ShapeDtypeStruct((64, 4, 2, 4,...  115 us
    unnamed x5, local copies, waits for them, and re-layouts  2.91 us

profile of v5, /device:TPU:1, one launch (start us, length us, event | category | flops | bytes accessed | tf_op | source)
XLA Modules:
  0.0 118.4 jit_solution(7195950841383471766)
XLA Ops:
  0.0 0.0 copy-start
  0.0 1.2 %copy-done = f32[64,4,8,128]{3,2,1,0:T(8,128)S(1)} copy-done((f32[64,4,8,128]{3,2,1,0:T(8,128)S(1)}, f32[64,4,8,128]{3,2,1,0:T(8,128)}, u32[]{:S(2)}) %copy-start) | copy-done | bytes 1048600
  1.2 0.0 copy-start.1
  1.2 0.7 copy-done.1
  1.9 115.5 %shard_map.28 = f32[64,4,2,4,128]{4,3,2,1,0:T(4,128)S(1)} custom-call(f32[64,4,8,128]{3,2,1,0:T(8,128)S(1)} %copy-done, f32[4,8,128]{2,1,0:T(8,128)S(1)} %copy-done.1), custom_call_target="tpu_custom_call" | custom-call | tf_op jit(solution)/shard_map/pallas_call | solution.py:408
  117.4 1.0 copy.4
Async XLA Ops:
  0.0 1.2 %copy-start = (f32[64,4,8,128]{3,2,1,0:T(8,128)S(1)}, f32[64,4,8,128]{3,2,1,0:T(8,128)}, u32[]{:S(2)}) copy-start(f32[64,4,8,128]{3,2,1,0:T(8,128)} %orb_ref.1) | copy-start | bytes 3145732
  1.2 0.7 copy-start.1

commit v6 on v5

--- a/solution.py
+++ b/solution.py
@@ -327,25 +327,24 @@
             stage(p)
     core_swap(0).wait()
 
-    def rows_copy(to):
-        return remote(y_ref.at[pl.ds(64 * to, 64)], out_ref.at[:, z_hi, core], dsend, drecv, (me, to))
-
-    def keep(to):
-        return pltpu.make_async_copy(y_ref.at[pl.ds(64 * to, 64)], out_ref.at[:, z_hi, core], own.at[7])
-
-    def rotate_rows(b, half):
-        to = 2 * b + half
-        y = dot(w_ref[64 * half:64 * half + 64, :], x_ref[128 * b:128 * b + 128, :], NN)
+    def ends(to, first, count):
+        rows = y_ref.at[pl.ds(64 * to + first, count)]
+        return rows, out_ref.at[pl.ds(first, count), z_hi, core]
+
+    def rotate_rows(b, start, count):
+        to, first = 2 * b + start // 64, start % 64
+        y = dot(w_ref[start:start + count, :], x_ref[128 * b:128 * b + 128, :], NN)
         for q in range(4):
-            y_ref[64 * to:64 * to + 64, q, :] = y[:, 128 * q:128 * q + 128]
+            y_ref[128 * b + start:128 * b + start + count, q, :] = y[:, 128 * q:128 * q + 128]
+        rows, place = ends(to, first, count)
 
         @pl.when(my_orb != to)
         def _():
-            rows_copy(to).start()
+            remote(rows, place, dsend, drecv, (me, to)).start()
 
         @pl.when(my_orb == to)
         def _():
-            keep(to).start()
+            pltpu.make_async_copy(rows, place, own.at[7]).start()
         return y
 
     soon, later = [], []
@@ -356,8 +355,11 @@
             while work:
                 work.pop(0)()
 
-        factor_block(a_ref, w_ref, 128 * COLUMN[b], {
-            0: lambda: run(soon), 7: lambda: tops.append(rotate_rows(b, 0)), 8: lambda: run(later)})
+        count = 32 if b == 3 else 64
+        after = {0: lambda: run(soon), 8: lambda: run(later)}
+        for start in range(0, 128 - count, count):
+            after[(start + count) // 8 - 1] = lambda start=start: tops.append(rotate_rows(b, start, count))
+        factor_block(a_ref, w_ref, 128 * COLUMN[b], after)
         w = w_ref[...]
         if b == 0:
             core_swap(1).wait()
@@ -372,7 +374,8 @@
         if b < 3:
             lower(b + 1)
             update(b + 1, b + 1)
-        y = jnp.concatenate([tops[0], rotate_rows(b, 1)], axis=0)
+        tops.append(rotate_rows(b, 128 - count, count))
+        y = jnp.concatenate(tops, axis=0) if b < 3 else None
 
         def solve(i, y=y, low=low):
             rows = slice(128 * i, 128 * i + 128)
@@ -394,7 +397,7 @@
     for p in range(2):
         wait_bytes(parts[p].at[pl.ds(0, 15)], rsend.at[p])
         wait_bytes(zparts[p].at[pl.ds(0, 7)], zsend.at[p])
-    keep(0).wait()
+    wait_bytes(y_ref.at[pl.ds(0, 64)], own.at[7])
     wait_bytes(y_ref.at[pl.ds(0, 448)], dsend)
     wait_bytes(y_ref.at[pl.ds(0, 448)], drecv)
 
@@ -416,7 +419,7 @@
                         dma((2,)), dma((2,)), dma, dma, dma((2, 2)), dma((2, 2)), dma((2,)), dma((2,)), dma((8,)),
                         dma((2,)), dma((2,)), dma((2,)), dma((2,)), dma((2,)), dma((2,)),
                         dma((2,)), dma((2,)), dma((3,)), dma((3,)), dma, dma],
-        compiler_params=pltpu.CompilerParams(collective_id=1, has_side_effects=True, vmem_limit_bytes=32 << 20),
+        compiler_params=pltpu.CompilerParams(collective_id=1, has_side_effects=True, vmem_limit_bytes=52 << 20),
     )(orbitals, potential)
 
 

time: 119 us -> 117 us (0.983)
  local copies, waits for them, and re-layouts: 2.91 us -> 1.69 us
    unnamed x5 -> x3, local copies, waits for them, and re-layouts: 2.91 us -> 1.69 us
where the time goes in v6:
time: 117 us
  Pallas kernels  115 us (98%)
  local copies, waits for them, and re-layouts  1.69 us (1%)
    pallas_call x1, Pallas kernels, mega(): pl.pallas_call(mega_kernel, out_shape=jax.ShapeDtypeStruct((64, 4, 2, 4,...  115 us

profile of v6, /device:TPU:1, one launch (start us, length us, event | category | flops | bytes accessed | tf_op | source)
XLA Modules:
  0.0 116.8 jit_solution(11842379200877583248)
XLA Ops:
  0.0 0.0 copy-start
  0.0 0.7 copy-done
  0.7 115.1 %shard_map.28 = f32[64,4,2,4,128]{4,3,2,1,0:T(4,128)S(1)} custom-call(f32[64,4,8,128]{3,2,1,0:T(8,128)} %orb_ref.1, f32[4,8,128]{2,1,0:T(8,128)S(1)} %copy-done), custom_call_target="tpu_custom_call" | custom-call | tf_op jit(solution)/shard_map/pallas_call | solution.py:411
  115.8 1.0 copy.4
Async XLA Ops:
  0.0 0.7 copy-start

commit v7 on v6

--- a/solution.py
+++ b/solution.py
@@ -134,7 +134,7 @@
     def body(d, carry):
         do(d)
         return carry
-    lax.fori_loop(first, last, body, 0)
+    lax.fori_loop(first, last, body, 0, unroll=True)
 
 
 def wait_bytes(like, sem):

time: 117 us -> 116 us (level)
  no operation moved by 1% of the time
where the time goes in v7:
time: 116 us
  Pallas kernels  114 us (98%)
  local copies, waits for them, and re-layouts  1.69 us (1%)
    pallas_call x1, Pallas kernels, mega(): pl.pallas_call(mega_kernel, out_shape=jax.ShapeDtypeStruct((64, 4, 2, 4,...  114 us

profile of v7, /device:TPU:1, one launch (start us, length us, event | category | flops | bytes accessed | tf_op | source)
XLA Modules:
  0.0 115.8 jit_solution(15585482590976241727)
XLA Ops:
  0.0 0.0 copy-start
  0.0 0.7 copy-done
  0.7 114.1 %shard_map.28 = f32[64,4,2,4,128]{4,3,2,1,0:T(4,128)S(1)} custom-call(f32[64,4,8,128]{3,2,1,0:T(8,128)} %orb_ref.1, f32[4,8,128]{2,1,0:T(8,128)S(1)} %copy-done), custom_call_target="tpu_custom_call" | custom-call | tf_op jit(solution)/shard_map/pallas_call | solution.py:411
  114.8 1.0 copy.4
Async XLA Ops:
  0.0 0.7 copy-start

commit v8 on v7

--- a/solution.py
+++ b/solution.py
@@ -122,7 +122,7 @@
 
 
 COLUMN = (0, 4, 7, 9)
-PIECES = ((0, 16), (512, 24))
+PIECES = ((0, 40),)
 CELLS = 128.0 * 8.0 * 128.0
 
 
@@ -142,7 +142,7 @@
 
 
 def mega_kernel(orb_ref, pot_ref, out_ref, a, b, pot5, c, slab, m6, x_ref, g_ref, a_ref, y_ref, w_ref, cbuf,
-                parts0, parts1, zparts0, zparts1, send, recv, psend, precv, asend, arecv, bsend, brecv, own,
+                parts0, zparts0, send, recv, psend, precv, asend, arecv, bsend, brecv, own,
                 csend, crecv, rsend, rrecv, zsend, zrecv, gsend, grecv, esend, erecv, dsend, drecv):
     me, my_orb = lax.axis_index("grid"), lax.axis_index("orb")
     xy, z_lo = me // 2, lax.rem(me, 2)
@@ -150,7 +150,7 @@
     z = z_hi * 2 + z_lo
     zc = z * 2 + core
     pot = pot5.reshape(128, 8, 128)
-    parts, zparts = (parts0, parts1), (zparts0, zparts1)
+    parts, zparts = (parts0,), (zparts0,)
     partner = (me, z_hi * 2 + 1 - core)
 
     def stack(i):
@@ -317,14 +317,11 @@
         wait_bytes(parts[p].at[pl.ds(0, 15)], gsend.at[p])
         core_swap(p).start()
 
-    gram(0)
+    for j in range(4):
+        gram(j)
     core_copy(0).start()
-    for j in range(1, 4):
-        gram(j)
-    core_copy(1).start()
     for stage in (start_scatter, start_exchange, start_gather, start_swap):
-        for p in range(2):
-            stage(p)
+        stage(0)
     core_swap(0).wait()
 
     def ends(to, first, count):
@@ -361,8 +358,6 @@
             after[(start + count) // 8 - 1] = lambda start=start: tops.append(rotate_rows(b, start, count))
         factor_block(a_ref, w_ref, 128 * COLUMN[b], after)
         w = w_ref[...]
-        if b == 0:
-            core_swap(1).wait()
         low = {}
 
         def lower(i, b=b, w=w, low=low):
@@ -394,7 +389,7 @@
         for s in range(2):
             wait_bytes(slab.at[k, pl.ds(0, 15), pl.ds(0, 4)], asend.at[k, s])
         wait_bytes(slab.at[k, pl.ds(0, 15)], bsend.at[k])
-    for p in range(2):
+    for p in range(1):
         wait_bytes(parts[p].at[pl.ds(0, 15)], rsend.at[p])
         wait_bytes(zparts[p].at[pl.ds(0, 7)], zsend.at[p])
     wait_bytes(y_ref.at[pl.ds(0, 64)], own.at[7])
@@ -415,7 +410,7 @@
         scratch_shapes=[vmem(2, 136, 8, 128), vmem(2, 136, 8, 128), vmem(32, 2, 2, 8, 128), vmem(2, 128, 2, 4, 128),
                         vmem(2, 16, 8, 2, 4, 128), vmem(8, 16, 2, 2, 4, 128),
                         vmem(512, 512), vmem(1280, 128), vmem(1280, 128), vmem(512, 4, 128), vmem(128, 128),
-                        vmem(640, 128), vmem(16, 16, 128), vmem(16, 24, 128), vmem(8, 16, 128), vmem(8, 24, 128),
+                        vmem(640, 128), vmem(16, 40, 128), vmem(8, 40, 128),
                         dma((2,)), dma((2,)), dma, dma, dma((2, 2)), dma((2, 2)), dma((2,)), dma((2,)), dma((8,)),
                         dma((2,)), dma((2,)), dma((2,)), dma((2,)), dma((2,)), dma((2,)),
                         dma((2,)), dma((2,)), dma((3,)), dma((3,)), dma, dma],

time: 116 us -> 121 us (1.043)
  Pallas kernels: 114 us -> 119 us
    pallas_call x1, Pallas kernels: 114 us -> 119 us  [mega(): pl.pallas_call(mega_kernel, out_shape=jax.ShapeDtypeStruct((64, 4, 2, 4,...]
where the time goes in v8:
time: 121 us
  Pallas kernels  119 us (98%)
  local copies, waits for them, and re-layouts  1.69 us (1%)
    pallas_call x1, Pallas kernels, mega(): pl.pallas_call(mega_kernel, out_shape=jax.ShapeDtypeStruct((64, 4, 2, 4,...  119 us

profile of v8, /device:TPU:1, one launch (start us, length us, event | category | flops | bytes accessed | tf_op | source)
XLA Modules:
  0.0 120.7 jit_solution(3588450549843709748)
XLA Ops:
  0.0 0.0 copy-start
  0.0 0.7 copy-done
  0.7 119.0 %shard_map.28 = f32[64,4,2,4,128]{4,3,2,1,0:T(4,128)S(1)} custom-call(f32[64,4,8,128]{3,2,1,0:T(8,128)} %orb_ref.1, f32[4,8,128]{2,1,0:T(8,128)S(1)} %copy-done), custom_call_target="tpu_custom_call" | custom-call | tf_op jit(solution)/shard_map/pallas_call | solution.py:406
  119.7 1.0 copy.4
Async XLA Ops:
  0.0 0.7 copy-start
